TPU v7x, 32 devices: a whole 2x2x4 slice. The times are simulated.
32 devices in a mesh: replica: 8 (over y, x, core), shard: 4 (over z).
Axes of the slice: x: 2, y: 2, z: 4, core: 2. Of those that a mesh axis runs over, the one named last changes fastest.
Arguments:
- hidden_in: bfloat16 [6144, 2048], P(('replica', 'shard')), may hold values from -6 to 6
- attention_gain: bfloat16 [2048], P('shard'), may hold values from 0.5 to 1.5
- query_weight: bfloat16 [2048, 2048], P('shard'), may hold values from -0.1875 to 0.1875
- key_weight: bfloat16 [2048, 256], P('shard'), may hold values from -0.1875 to 0.1875
- value_weight: bfloat16 [2048, 256], P('shard'), may hold values from -0.125 to 0.125
- output_weight: bfloat16 [2048, 2048], P('shard'), may hold values from -0.75 to 0.75
- feedforward_gain: bfloat16 [2048], P('shard'), may hold values from 0.5 to 1.5
- gate_weight: bfloat16 [2048, 5632], P('shard'), may hold values from -0.125 to 0.125
- up_weight: bfloat16 [2048, 5632], P('shard'), may hold values from -0.125 to 0.125
- down_weight: bfloat16 [5632, 2048], P('shard'), may hold values from -0.078125 to 0.078125
- out_grad: bfloat16 [6144, 2048], P(('replica', 'shard')), may hold values from -6 to 6
Outputs:
- output: bfloat16 [6144, 2048], P(('replica', 'shard'))
- grad_input: bfloat16 [6144, 2048], P(('replica', 'shard'))
- grad_attention_gain: float32 [2048], P('shard')
- grad_query_weight: float32 [2048, 2048], P('shard')
- grad_key_weight: float32 [2048, 256], P('shard')
- grad_value_weight: float32 [2048, 256], P('shard')
- grad_output_weight: float32 [2048, 2048], P('shard')
- grad_feedforward_gain: float32 [2048], P('shard')
- grad_gate_weight: float32 [2048, 5632], P('shard')
- grad_up_weight: float32 [2048, 5632], P('shard')
- grad_down_weight: float32 [5632, 2048], P('shard')
All inputs are finite; a program needn't handle non-finite values.
Results may differ from a plain program's by a relative error of at most 0.022.
Values may be sent and summed in bfloat16 or wider, within the bound.
No kernel may reach another device: no remote copies, remote signals or barrier semaphores. Data moves between devices by JAX's collectives and lax.ppermute only.
A program may use at most 448 MiB of HBM per device.

v0:
```python
import functools

import jax
import jax.numpy as jnp
from jax import lax
from jax.experimental import pallas as pl
from jax.experimental.pallas import tpu as pltpu
from jax.sharding import PartitionSpec as P

HEADS = 32
KV_HEADS = 4
HEAD = 64
GROUP = HEADS // KV_HEADS
CHIPS = 4
PIECES = 2 * CHIPS
PAIR = 2
LANES = 128

norm_eps = 1e-05
rope_base = 10000.0
masked_score = -1e30

f32 = jnp.float32
bf16 = jnp.bfloat16
VMEM = pltpu.VMEM
NT = (((1,), (1,)), ((), ()))
TN = (((0,), (0,)), ((), ()))


def dot(left, right):
    return jnp.dot(left, right, preferred_element_type=f32)


def dot_nt(left, right):
    return lax.dot_general(left, right, NT, preferred_element_type=f32)


def dot_tn(left, right):
    return lax.dot_general(left, right, TN, preferred_element_type=f32)


def shape(dims, kind):
    return jax.ShapeDtypeStruct(dims, kind)


def whole():
    return pl.BlockSpec(memory_space=VMEM)


TIMES = {"attention_back": 13.0}


def kernel_call(body, out_shape, in_specs, out_specs, operands, *, index=None, grid=(), scratch=(),
                aliases=None, name=None):
    params = pltpu.CompilerParams(
        vmem_limit_bytes=52 * 2**20, dimension_semantics=("arbitrary",) * len(grid)
    )
    moved = int(TIMES.get(name, 0.0) * 3.69e6)
    cost = pl.CostEstimate(flops=0, bytes_accessed=moved, transcendentals=0)
    common = dict(
        out_shape=out_shape,
        compiler_params=params,
        cost_estimate=cost,
        input_output_aliases=aliases or {},
        name=name,
    )
    if index is None:
        spec = pl.GridSpec(grid=grid, in_specs=in_specs, out_specs=out_specs, scratch_shapes=scratch)
        return pl.pallas_call(body, grid_spec=spec, **common)(*operands)
    spec = pltpu.PrefetchScalarGridSpec(
        num_scalar_prefetch=1, grid=grid, in_specs=in_specs, out_specs=out_specs,
        scratch_shapes=scratch,
    )
    return pl.pallas_call(body, grid_spec=spec, **common)(index, *operands)


def swap(value, mask):
    size = lax.axis_size("replica")
    return lax.ppermute(value, "replica", [(i, i ^ mask) for i in range(size)])


def shift(value, step):
    size = lax.axis_size("shard")
    pairs = [(i, i + step) for i in range(size) if 0 <= i + step < size]
    return lax.ppermute(value, "shard", pairs)


def plane_gather(value):
    return [value] + [swap(value, 2 * m) for m in range(1, CHIPS)]


def plane_gather_forward(value, *before):
    middle = value.shape[0] // 2
    across, along = swap(value, 2), swap(value, 4)
    if before:
        across, along = after(across, *before), after(along, *before)
    return [value, across, along, swap(across[:middle], 4), swap(along[middle:], 2)]


def plane_send(parts):
    return [parts[0]] + [swap(parts[m], 2 * m) for m in range(1, len(parts))]


def group_of(chip):
    return 2 * (chip & 1) + (chip >> 1)


def after(value, *others):
    return lax.optimization_barrier((value, *others))[0]


def attention_block_body(local, group_shards, index, q, k, v, o, gain, out, wo_out):
    scale = gain[:, :1]
    q_width = GROUP * HEAD
    cut = local // CHIPS
    for chip in range(CHIPS):

        group = group_of(chip)

        @pl.when(index[0] == chip)
        def _(group=group):
            parts = []
            for m in range(CHIPS):
                for s in range(group_shards):
                    start = group * q_width + s * local + (m ^ chip) * cut
                    parts.append(q[:, start : start + cut])
            parts.append(k[:, group * HEAD : (group + 1) * HEAD])
            parts.append(v[:, group * HEAD : (group + 1) * HEAD])
            wide = jnp.concatenate([part.astype(f32) for part in parts], axis=1)
            out[...] = (wide * scale).astype(bf16)

    half = local // 2
    shards = o.shape[1] // local
    for core in range(2):

        @pl.when(index[1] == core)
        def _():
            for s in range(shards):
                piece = o[:, s * local + core * half : s * local + (core + 1) * half]
                wo_out[:, s * half : (s + 1) * half] = piece


def attention_block(index, query, key, value, output, gain):
    local, width = query.shape
    half = local // 2
    shards = width // local
    return kernel_call(
        functools.partial(attention_block_body, local, shards // CHIPS),
        (
            shape((half, GROUP * HEAD + 2 * HEAD), bf16),
            shape((local // CHIPS, width // 2), bf16),
        ),
        [
            pl.BlockSpec((half, width), lambda i, n: (n[1], 0)),
            pl.BlockSpec((half, key.shape[1]), lambda i, n: (n[1], 0)),
            pl.BlockSpec((half, key.shape[1]), lambda i, n: (n[1], 0)),
            pl.BlockSpec((local // CHIPS, width), lambda i, n: (n[0], 0)),
            pl.BlockSpec((half, LANES), lambda i, n: (n[1], 0)),
        ],
        (
            pl.BlockSpec((half, GROUP * HEAD + 2 * HEAD), lambda i, n: (0, 0)),
            pl.BlockSpec((local // CHIPS, width // 2), lambda i, n: (0, 0)),
        ),
        (query, key, value, output, gain),
        index=index,
        grid=(1,),
        name="attention_block",
    )


def feedforward_block_body(ff_local, cut, index, gate, up, gain, out):
    scale = gain[:, :1]
    shards = gate.shape[1] // ff_local
    width = shards * cut
    for chip in range(CHIPS):

        @pl.when(index[0] == chip)
        def _():
            for n, source in enumerate((gate, up)):
                parts = [
                    source[:, s * ff_local + chip * cut : s * ff_local + (chip + 1) * cut].astype(f32)
                    for s in range(shards)
                ]
                wide = jnp.concatenate(parts, axis=1)
                out[:, n * width : (n + 1) * width] = (wide * scale).astype(bf16)


def feedforward_block(index, gate, up, gain, ff_local):
    local, ff = gate.shape
    half = local // 2
    rows = 64
    steps = half // rows
    cut = ff_local // CHIPS
    width = 2 * (ff // CHIPS)
    return kernel_call(
        functools.partial(feedforward_block_body, ff_local, cut),
        shape((half, width), bf16),
        [
            pl.BlockSpec((rows, ff), lambda i, n: (n[1] * steps + i, 0)),
            pl.BlockSpec((rows, ff), lambda i, n: (n[1] * steps + i, 0)),
            pl.BlockSpec((rows, LANES), lambda i, n: (n[1] * steps + i, 0)),
        ],
        pl.BlockSpec((rows, width), lambda i, n: (i, 0)),
        (gate, up, gain),
        index=index,
        grid=(steps,),
        name="feedforward_block",
    )


def own_first_body(local, index, *refs):
    count = len(refs) // 2
    half = local // 2
    for core in range(2):

        @pl.when(index[1] == core)
        def _():
            for source, out in zip(refs[:count], refs[count:]):
                shards = source.shape[1] // local
                sides = out.shape[1] // (shards * half)
                for side in range(sides):
                    for s in range(shards):
                        start = s * local + (core ^ side) * half
                        spot = (side * shards + s) * half
                        out[:, spot : spot + half] = source[:, start : start + half]


def own_first(index, sources, local, halves=2):
    return kernel_call(
        functools.partial(own_first_body, local),
        tuple(shape((v.shape[0], v.shape[1] * halves // 2), bf16) for v in sources),
        [pl.BlockSpec(v.shape, lambda i, n: (0, 0)) for v in sources],
        tuple(
            pl.BlockSpec((v.shape[0], v.shape[1] * halves // 2), lambda i, n: (0, 0)) for v in sources
        ),
        tuple(sources),
        index=index,
        grid=(1,),
        name="own_first",
    )


def down_block_body(local, index, source, out):
    own_first_body(local, index, source, out)


def down_block(index, down, local):
    ff_local, width = down.shape
    cut = ff_local // CHIPS
    return kernel_call(
        functools.partial(down_block_body, local),
        shape((cut, width // 2), bf16),
        [pl.BlockSpec((cut, width), lambda i, n: (n[0], 0))],
        pl.BlockSpec((cut, width // 2), lambda i, n: (0, 0)),
        (down,),
        index=index,
        grid=(1,),
        name="down_block",
    )


def part_sum(parts):
    total = parts[0][...]
    for part in parts[1:]:
        total = total + part[...].astype(f32)
    return total


def mean_of(values):
    return jnp.mean(values, axis=1, keepdims=True)


def middle_body(*refs):
    parts, (x, middle, two) = refs[:PAIR], refs[PAIR:]
    total = x[...].astype(f32) + part_sum(parts)
    middle[...] = total
    two[...] = (total * lax.rsqrt(mean_of(total * total) + norm_eps)).astype(bf16)


def middle_call(parts, x):
    return kernel_call(
        middle_body,
        (shape(x.shape, f32), shape(x.shape, bf16)),
        [whole()] * (PAIR + 1),
        (whole(), whole()),
        (*parts, x),
        name="middle",
    )


def norm_back(e, values):
    inverse = lax.rsqrt(mean_of(values * values) + norm_eps)
    return inverse * e - values * (inverse * inverse * inverse) * mean_of(e * values)


def grad_middle_body(*refs):
    parts, (middle, g, grad, low) = refs[:CHIPS], refs[CHIPS:]
    total = g[...].astype(f32) + norm_back(part_sum(parts), middle[...])
    grad[...] = total
    low[...] = total.astype(bf16)


def grad_middle_call(parts, middle, g):
    return kernel_call(
        grad_middle_body,
        (shape(g.shape, f32), shape(g.shape, bf16)),
        [whole()] * (CHIPS + 2),
        (whole(), whole()),
        (*parts, middle, g),
        name="grad_middle",
    )


def store_in_order(local, index, value, out):
    half = local // 2
    shards = out.shape[1] // local
    for core in range(2):

        @pl.when(index[1] == core)
        def _():
            for side in range(2):
                for s in range(shards):
                    spot = s * local + (core ^ side) * half
                    start = (side * shards + s) * half
                    out[:, spot : spot + half] = value[:, start : start + half].astype(bf16)


def output_body(local, index, *refs):
    parts, (middle, out) = refs[:CHIPS], refs[CHIPS:]
    store_in_order(local, index, middle[...] + part_sum(parts), out)


def output_call(index, parts, middle, local):
    spec = pl.BlockSpec(middle.shape, lambda i, n: (0, 0))
    return kernel_call(
        functools.partial(output_body, local),
        shape(middle.shape, bf16),
        [spec] * (CHIPS + 1),
        spec,
        (*parts, middle),
        index=index,
        grid=(1,),
        name="output",
    )


def grad_input_body(local, index, *refs):
    parts, (x, grad, out) = refs[:PAIR], refs[PAIR:]
    total = grad[...] + norm_back(part_sum(parts), x[...].astype(f32))
    store_in_order(local, index, total, out)


def grad_input_call(index, parts, x, grad, local):
    spec = pl.BlockSpec(x.shape, lambda i, n: (0, 0))
    return kernel_call(
        functools.partial(grad_input_body, local),
        shape(x.shape, bf16),
        [spec] * (PAIR + 2),
        spec,
        (*parts, x, grad),
        index=index,
        grid=(1,),
        name="grad_input",
    )


def grad_qkv_body(shards, grad_q, first, *refs):
    rest, (cosine, sine), outs = refs[: shards - 1], refs[shards - 1 : shards + 1], refs[shards + 1 :]
    total = first[...]
    for term in rest:
        total = total + term[...].astype(f32)
    rows = cosine.shape[1]
    width = GROUP * HEAD
    cos, sin = cosine[...], sine[...]
    for n, out in enumerate(outs):
        out[:, :width] = grad_q[:, n * width : (n + 1) * width]
        for m in range(PAIR):
            span = slice(m * rows, (m + 1) * rows)
            turned = total[span, n * 2 * HEAD : (n + 1) * 2 * HEAD].T
            k = turned[:HEAD]
            k = k * cos - half_rotated(k) * sin
            both = jnp.concatenate([k, turned[HEAD:]], axis=0)
            out[span, width:] = both.T.astype(bf16)


def grad_qkv_call(grad_q, first, rest, cosine, sine):
    tokens = grad_q.shape[0]
    return kernel_call(
        functools.partial(grad_qkv_body, len(rest) + 1),
        (shape((tokens, GROUP * HEAD + 2 * HEAD), bf16),) * PAIR,
        [whole()] * (len(rest) + 4),
        (whole(),) * PAIR,
        (grad_q, first, *rest, cosine, sine),
        name="grad_qkv",
    )


def out_sends_body(index, term, *outs):
    cut = outs[0].shape[0] // PAIR
    for row in range(2):

        @pl.when(index[0] >> 1 == row)
        def _():
            for n in range(PAIR):
                for m in range(CHIPS):
                    spot = (n * CHIPS + m) * cut
                    start = (n ^ row) * cut
                    outs[m ^ (2 * n)][start : start + cut, :] = term[spot : spot + cut, :]


def out_sends(index, term):
    rows, width = term.shape
    rows //= CHIPS
    return kernel_call(
        out_sends_body,
        (shape((rows, width), bf16),) * CHIPS,
        [pl.BlockSpec(term.shape, lambda i, n: (0, 0))],
        (pl.BlockSpec((rows, width), lambda i, n: (0, 0)),) * CHIPS,
        (term,),
        index=index,
        grid=(1,),
        name="out_sends",
    )


def out_block_body(shards, index, *refs):
    parts, out = refs[:CHIPS], refs[CHIPS]
    group_shards = shards // CHIPS
    cut = parts[0].shape[0] // (PAIR * group_shards)
    sums = [parts[m][...].astype(f32) + parts[m + 2][...].astype(f32) for m in range(2)]
    for side in range(2):

        @pl.when(index[0] & 1 == side)
        def _():
            for m in range(2):
                for n in range(PAIR * group_shards):
                    shard = (m ^ side) * PAIR * group_shards + n
                    rows = sums[m][n * cut : (n + 1) * cut].astype(bf16)
                    out[2 * shard * cut : (2 * shard + 1) * cut, :] = rows[:, :512]
                    out[(2 * shard + 1) * cut : (2 * shard + 2) * cut, :] = rows[:, 512:]


def out_block_call(index, parts, shards):
    rows, width = parts[0].shape
    return kernel_call(
        functools.partial(out_block_body, shards),
        shape((2 * PAIR * rows, width // 2), bf16),
        [pl.BlockSpec((rows, width), lambda i, n: (0, 0))] * CHIPS,
        pl.BlockSpec((2 * PAIR * rows, width // 2), lambda i, n: (0, 0)),
        tuple(parts),
        index=index,
        grid=(1,),
        name="out_block",
    )


def half_rotated(values):
    middle = values.shape[0] // 2
    return jnp.concatenate([-values[middle:], values[:middle]], axis=0)


def qkv_body(make, *refs):
    if make:
        xs, (own, other, cosine, sine, queries, kv, xhat) = refs[:PAIR], refs[PAIR:]
        rows, width = xs[0].shape
        for m in range(PAIR):
            x = xs[m][...].astype(f32)
            inverse = lax.rsqrt(mean_of(x * x) + norm_eps)
            xhat[m * rows : (m + 1) * rows, :] = (x * inverse).astype(bf16)
    else:
        xhat, own, other, cosine, sine, queries, kv = refs
        rows, width = cosine.shape[1], xhat.shape[1]
    cos, sin = cosine[...], sine[...]
    total = dot(xhat[:, : width // 2], own[...]) + dot(xhat[:, width // 2 :], other[...])
    for m in range(PAIR):
        turned = total[m * rows : (m + 1) * rows].T
        for h in range(GROUP + 1):
            u = turned[h * HEAD : (h + 1) * HEAD]
            u = u * cos + half_rotated(u) * sin
            if h < GROUP:
                queries[m, :, h * rows : (h + 1) * rows] = (u * HEAD ** (-0.5)).astype(bf16)
            else:
                both = jnp.concatenate([u, turned[(h + 1) * HEAD :]], axis=0)
                kv[m * rows : (m + 1) * rows, :] = both.T.astype(bf16)


def qkv_call(xs, own, other, cosine, sine):
    make = isinstance(xs, list)
    rows = cosine.shape[1]
    tokens = PAIR * rows
    outs = (shape((PAIR, HEAD, GROUP * rows), bf16), shape((tokens, 2 * HEAD), bf16))
    if make:
        outs = outs + (shape((tokens, xs[0].shape[1]), bf16),)
    operands = (*(xs if make else (xs,)), own, other, cosine, sine)
    return kernel_call(
        functools.partial(qkv_body, make),
        outs,
        [whole()] * len(operands),
        tuple(whole() for _ in outs),
        operands,
        name="qkv",
    )


def out_rows_body(index, *refs):
    pieces, out = refs[:CHIPS], refs[CHIPS]
    cut = pieces[0].shape[0] // PAIR
    for row in range(2):

        @pl.when(index[0] >> 1 == row)
        def _():
            for n in range(PAIR):
                for m in range(CHIPS):
                    spot = (n * CHIPS + m) * cut
                    start = (n ^ row) * cut
                    out[spot : spot + cut, :] = pieces[m ^ (2 * n)][start : start + cut, :]


def out_rows_call(index, pieces):
    rows, width = pieces[0].shape
    return kernel_call(
        out_rows_body,
        shape((CHIPS * rows, width), bf16),
        [pl.BlockSpec((rows, width), lambda i, n: (0, 0))] * CHIPS,
        pl.BlockSpec((CHIPS * rows, width), lambda i, n: (0, 0)),
        tuple(pieces),
        index=index,
        grid=(1,),
        name="out_rows",
    )


LANE_HEADS = 4


def own_block_bias(rows):
    key = lax.broadcasted_iota(jnp.int32, (rows, rows), 0)
    mine = lax.broadcasted_iota(jnp.int32, (rows, rows), 1)
    return jnp.where(key <= mine, 0.0, masked_score)


def set_bias(bias):
    rows = bias.shape[0]
    value = own_block_bias(rows)
    for h in range(LANE_HEADS):
        bias[:, h * rows : (h + 1) * rows] = value


def far_bias(depth, d):
    return jnp.where(d <= depth, 0.0, masked_score) if d else 0.0


def attention_body(shards, index, queries, *refs):
    kvs = refs[:shards]
    turned_out, out, stats, bias, terms, out_turned = refs[shards:]
    rows = bias.shape[0]
    wide = LANE_HEADS * rows

    @pl.when(pl.program_id(0) == 0)
    def _():
        set_bias(bias)

    ks = [kv[:, :HEAD] for kv in kvs]
    v_turned = jnp.concatenate([kv[...] for kv in kvs], axis=0).astype(f32).T[HEAD:].astype(bf16)
    for n in range(GROUP // LANE_HEADS):
        span = slice(n * wide, (n + 1) * wide)
        q = queries[0, :, span]
        scores, top = [], None
        for d in range(shards):
            score = dot(ks[d], q)
            if d == 0:
                score = score + bias[...]
            scores.append(score)
            highest = jnp.max(score, axis=0, keepdims=True) + far_bias(index[2], d)
            top = highest if top is None else jnp.maximum(top, highest)
        total = None
        for d in range(shards):
            term = jnp.exp(scores[d] - (top - far_bias(index[2], d)))
            part = jnp.sum(term, axis=0, keepdims=True)
            total = part if total is None else total + part
            terms[d * rows : (d + 1) * rows, :] = term.astype(bf16)
        out_turned[:, span] = dot(v_turned, terms[...]) / total
        stats[0, :, span] = top + jnp.log(total)
    turned_out[0] = out_turned[...].astype(bf16)
    straight = out_turned[...].T
    for h in range(GROUP):
        out[:, h * HEAD : (h + 1) * HEAD] = straight[h * rows : (h + 1) * rows].astype(bf16)


def attention_call(index, queries, kvs):
    chips, _, wide = queries.shape
    rows = wide // GROUP
    shards = len(kvs)
    keys = shards * rows
    block = pl.BlockSpec((1, HEAD, wide), lambda i, n: (i, 0, 0))
    return kernel_call(
        functools.partial(attention_body, shards),
        (
            shape((chips, HEAD, wide), bf16),
            shape((chips * rows, GROUP * HEAD), bf16),
            shape((chips, 1, wide), f32),
        ),
        [block] + [pl.BlockSpec((rows, 2 * HEAD), lambda i, n: (i, 0))] * shards,
        (
            block,
            pl.BlockSpec((rows, GROUP * HEAD), lambda i, n: (i, 0)),
            pl.BlockSpec((1, 1, wide), lambda i, n: (i, 0, 0)),
        ),
        (queries, *kvs),
        index=index,
        grid=(chips,),
        scratch=(
            VMEM((rows, LANE_HEADS * rows), f32),
            VMEM((keys, LANE_HEADS * rows), bf16),
            VMEM((HEAD, wide), f32),
        ),
        name="attention",
    )


def attention_back_body(shards, index, branch, wo_own, wo_other, cosine, sine, *refs):
    per_group = 3 + shards
    inputs = [refs[n * per_group : (n + 1) * per_group] for n in range(PAIR)]
    grad_q, grad_first, grad_rest = refs[-7:-4]
    bias, probs_low, grads_low, grad_lanes = refs[-4:]
    rows = bias.shape[0]
    wide = LANE_HEADS * rows
    width = branch.shape[1]
    set_bias(bias)
    cos, sin = cosine[...], sine[...]
    for n, (queries, turned_out, stats, *kvs) in enumerate(inputs):
        heads = slice(n * GROUP * HEAD, (n + 1) * GROUP * HEAD)
        grad_out = dot_nt(wo_own[heads, :], branch[:, : width // 2])
        grad_out = grad_out + dot_nt(wo_other[heads, :], branch[:, width // 2 :])
        for h in range(GROUP):
            grad_lanes[:, h * rows : (h + 1) * rows] = grad_out[h * HEAD : (h + 1) * HEAD].astype(bf16)
        ks = [kv[:, :HEAD] for kv in kvs]
        vs = [kv[:, HEAD:] for kv in kvs]
        k_turned = jnp.concatenate([kv[...] for kv in kvs], axis=0).astype(f32).T[:HEAD].astype(bf16)
        k_total, v_total, parts = None, None, []
        for c in range(GROUP // LANE_HEADS):
            span = slice(c * wide, (c + 1) * wide)
            q, mine = queries[0, :, span], grad_lanes[:, span]
            delta = jnp.sum(
                mine.astype(f32) * turned_out[0, :, span].astype(f32), axis=0, keepdims=True
            )
            for d in range(shards):
                score = dot(ks[d], q)
                if d == 0:
                    score = score + bias[...]
                probs = jnp.exp(score - (stats[0, :, span] - far_bias(index[2], d)))
                grad_scores = probs * (dot(vs[d], mine) - delta)
                probs_low[d * rows : (d + 1) * rows, :] = probs.astype(bf16)
                grads_low[d * rows : (d + 1) * rows, :] = grad_scores.astype(bf16)
            u = dot(k_turned, grads_low[...]) * HEAD ** (-0.5)
            parts.append(u * cos - half_rotated(u) * sin)
            k_term = dot_nt(grads_low[...], q)
            v_term = dot_nt(probs_low[...], mine)
            k_total = k_term if k_total is None else k_total + k_term
            v_total = v_term if v_total is None else v_total + v_term
        straight = jnp.concatenate(parts, axis=1).T
        for h in range(GROUP):
            spot = (n * GROUP + h) * HEAD
            grad_q[:, spot : spot + HEAD] = straight[h * rows : (h + 1) * rows].astype(bf16)
        both = jnp.concatenate([k_total, v_total], axis=1)
        spot = slice(n * 2 * HEAD, (n + 1) * 2 * HEAD)
        grad_first[:, spot] = both[:rows, :]
        for d in range(1, shards):
            grad_rest[d - 1, :, spot] = both[d * rows : (d + 1) * rows, :].astype(bf16)


def attention_back_call(index, m, branch, wo_own, wo_other, cosine, sine, groups, before):
    chips, _, wide = groups[0][0].shape
    rows = wide // GROUP
    shards = len(groups[0][3])
    keys = shards * rows
    tokens = chips * rows
    block = pl.BlockSpec((1, HEAD, wide), lambda i, n: (m, 0, 0))
    in_specs = [whole()] * 5
    operands = [branch, wo_own, wo_other, jnp.tile(cosine, (1, LANE_HEADS)), jnp.tile(sine, (1, LANE_HEADS))]
    for queries, turned, stats, kvs in groups:
        in_specs += [block, block, pl.BlockSpec((1, 1, wide), lambda i, n: (m, 0, 0))]
        in_specs += [pl.BlockSpec((rows, 2 * HEAD), lambda i, n: (m, 0))] * shards
        operands += [queries, turned, stats, *kvs]
    aliases = {}
    if before is not None:
        aliases = {1 + len(operands) + n: n for n in range(3)}
        in_specs += [pl.BlockSpec(memory_space=pl.ANY)] * 3
        operands += list(before)
    outs = (
        shape((tokens, PAIR * GROUP * HEAD), bf16),
        shape((tokens, PAIR * 2 * HEAD), f32),
        shape((shards - 1, tokens, PAIR * 2 * HEAD), bf16),
    )
    out_specs = (
        pl.BlockSpec((rows, PAIR * GROUP * HEAD), lambda i, n: (m, 0)),
        pl.BlockSpec((rows, PAIR * 2 * HEAD), lambda i, n: (m, 0)),
        pl.BlockSpec((shards - 1, rows, PAIR * 2 * HEAD), lambda i, n: (0, m, 0)),
    )
    return kernel_call(
        functools.partial(attention_back_body, shards),
        outs,
        in_specs,
        out_specs,
        tuple(operands),
        index=index,
        grid=(1,),
        scratch=(
            VMEM((rows, LANE_HEADS * rows), f32),
            VMEM((keys, LANE_HEADS * rows), bf16),
            VMEM((keys, LANE_HEADS * rows), bf16),
            VMEM((HEAD, wide), bf16),
        ),
        aliases=aliases,
        name="attention_back",
    )


def parts_body(steps, transposed, count, *refs):
    lefts, owns, others = refs[:count], refs[count : 2 * count], refs[2 * count : 3 * count]
    outs = refs[3 * count :]
    rows = outs[0].shape[0]
    step = pl.program_id(0)

    def run(weights):
        total = None
        for left, weight in zip(lefts, weights):
            term = (dot_nt if transposed else dot)(left[...], weight[...])
            total = term if total is None else total + term
        for m, out in enumerate(outs):
            out[...] = total[m * rows : (m + 1) * rows, :].astype(out.dtype)

    @pl.when(step < steps)
    def _():
        run(owns)

    @pl.when(step >= steps)
    def _():
        run(others)


def parts_call(terms, rows, transposed, name):
    tokens = terms[0][0].shape[0]
    half = terms[0][1].shape[0] if transposed else terms[0][1].shape[1]
    tile = 256
    steps = half // tile
    last = steps - 1
    specs = [pl.BlockSpec((tokens, term[0].shape[1]), lambda j: (0, 0)) for term in terms]
    for side in range(2):
        for left, _, _, spot in terms:
            depth = left.shape[1]

            def place(side, spot, j):
                step = jnp.maximum(j - steps, 0) if side else jnp.minimum(j, last)
                return (step, spot) if transposed else (spot, step)

            block = (tile, depth) if transposed else (depth, tile)
            specs.append(pl.BlockSpec(block, functools.partial(place, side, spot)))
    count = tokens // rows
    return kernel_call(
        functools.partial(parts_body, steps, transposed, len(terms)),
        tuple(shape((rows, 2 * half), f32 if m == 0 else bf16) for m in range(count)),
        specs,
        tuple(pl.BlockSpec((rows, tile), lambda j: (0, j)) for _ in range(count)),
        (*(term[0] for term in terms), *(term[1] for term in terms), *(term[2] for term in terms)),
        grid=(2 * steps,),
        name=name,
    )


def gate_body(count, *refs):
    twos = refs[:count]
    gate_own, up_own, gate_other, up_other, act, for_gate, for_up, two_all = refs[count:]
    half = two_all.shape[1] // 2

    @pl.when(pl.program_id(0) == 0)
    def _():
        start = 0
        for two in twos:
            two_all[start : start + two.shape[0], :] = two[...]
            start += two.shape[0]

    own = jnp.concatenate([gate_own[...], up_own[...]], axis=1)
    other = jnp.concatenate([gate_other[...], up_other[...]], axis=1)
    both = dot(two_all[:, :half], own) + dot(two_all[:, half:], other)
    wide = gate_own.shape[1]
    gate, up = both[:, :wide], both[:, wide:]
    sig = 1.0 / (1.0 + jnp.exp(-gate))
    silu = gate * sig
    act[...] = (silu * up).astype(bf16)
    for_gate[...] = (up * sig * (1.0 + gate * (1.0 - sig))).astype(bf16)
    for_up[...] = silu.astype(bf16)


def gate_call(twos, own, other):
    rows, width = twos[0].shape
    tokens = CHIPS * rows
    half = width // 2
    ff = own.shape[1] // 2
    tile = LANES
    steps = ff // tile
    weight = [
        pl.BlockSpec((half, tile), lambda j: (0, j)),
        pl.BlockSpec((half, tile), lambda j: (0, j + steps)),
    ]
    column = pl.BlockSpec((tokens, tile), lambda j: (0, j))
    return kernel_call(
        functools.partial(gate_body, len(twos)),
        tuple(shape((tokens, ff), bf16) for _ in range(3)) + (shape((tokens, width), bf16),),
        [pl.BlockSpec(two.shape, lambda j: (0, 0)) for two in twos] + weight + weight,
        (column, column, column, pl.BlockSpec((tokens, width), lambda j: (0, 0))),
        (*twos, own, own, other, other),
        grid=(steps,),
        name="gate",
    )


def hidden_back_body(g, own, other, for_gate, for_up, grads):
    half = g.shape[1] // 2
    ff = own.shape[0]
    hidden = dot_nt(g[:, :half], own[...]) + dot_nt(g[:, half:], other[...])
    grads[:, :ff] = (hidden * for_gate[...].astype(f32)).astype(bf16)
    grads[:, ff:] = (hidden * for_up[...].astype(f32)).astype(bf16)


def hidden_back_call(g, own, other, for_gate, for_up):
    tokens, width = g.shape
    ff, half = own.shape
    block = tokens // 2
    row = lambda i: (i, 0)
    fixed = lambda i: (0, 0)
    return kernel_call(
        hidden_back_body,
        shape((tokens, 2 * ff), bf16),
        [
            pl.BlockSpec((block, width), row),
            pl.BlockSpec((ff, half), fixed),
            pl.BlockSpec((ff, half), fixed),
            pl.BlockSpec((block, ff), row),
            pl.BlockSpec((block, ff), row),
        ],
        pl.BlockSpec((block, 2 * ff), row),
        (g, own, other, for_gate, for_up),
        grid=(2,),
        name="hidden_back",
    )


def weight_grad_body(per, outputs, adds, left, right, *refs):
    added = [refs[n * outputs : (n + 1) * outputs] for n in range(adds)]
    outs, turned = refs[adds * outputs : -1], refs[-1]
    step = pl.program_id(0)

    @pl.when(step == 0)
    def _():
        turned[...] = left[...].T

    for n in range(outputs):

        @pl.when(step // per == n)
        def _(n=n):
            total = dot(turned[...], right[...])
            for terms in added:
                total = total + terms[n][...].astype(f32)
            outs[n][...] = total.astype(bf16)


def weight_grad(left, left_side, right, place, width, outputs, added, name):
    tokens = left.shape[0]
    rows = left.shape[1] // (1 if left_side is None else 2)
    tile = 256 if width % 256 == 0 else width
    per = width // tile
    first = place * width // tile
    side = left_side or 0

    def spot(n, j):
        return (0, jnp.clip(j - n * per, 0, per - 1))

    tiles = [pl.BlockSpec((rows, tile), functools.partial(spot, n)) for n in range(outputs)]
    return kernel_call(
        functools.partial(weight_grad_body, per, outputs, len(added)),
        tuple(shape((rows, width), bf16) for _ in range(outputs)),
        [
            pl.BlockSpec((tokens, rows), lambda j: (0, side)),
            pl.BlockSpec((tokens, tile), lambda j: (0, first + j)),
        ]
        + tiles * len(added),
        tuple(tiles),
        (left, right, *(term for terms in added for term in terms)),
        grid=(per * outputs,),
        scratch=(VMEM((rows, tokens), bf16),),
        name=name,
    )


def rows_result_body(local, index, *refs):
    pieces, out = refs[:PIECES], refs[PIECES]
    half = local // 2
    shards = out.shape[1] // local
    for m in range(CHIPS):
        for core in range(2):

            @pl.when((pl.program_id(0) == m) & (index[1] == core))
            def _():
                for side in range(2):
                    piece = pieces[2 * m + side]
                    for s in range(shards):
                        spot = s * local + (core ^ side) * half
                        out[:, spot : spot + half] = piece[:, s * half : (s + 1) * half].astype(f32)


def rows_result(index, pieces, local, name):
    cut, half_width = pieces[0].shape
    return kernel_call(
        functools.partial(rows_result_body, local),
        shape((CHIPS * cut, 2 * half_width), f32),
        [pl.BlockSpec((cut, half_width), lambda i, n: (0, 0))] * PIECES,
        pl.BlockSpec((cut, 2 * half_width), lambda i, n: (n[0] ^ i, 0)),
        tuple(pieces),
        index=index,
        grid=(CHIPS,),
        name=name,
    )


def out_result_body(local, base, index, *refs):
    pieces, out = refs[:PIECES], refs[PIECES]
    half = local // 2
    cut = local // CHIPS
    shards = out.shape[1] // local
    for m in range(CHIPS):
        for core in range(2):

            @pl.when((pl.program_id(0) == m) & (index[1] == core))
            def _():
                for side in range(2):
                    piece = pieces[2 * m + side]
                    for s in range(shards):
                        spot = s * local + (core ^ side) * half
                        row, column = (0, s * half) if s * half < 512 else (cut, s * half - 512)
                        column += base
                        out[:, spot : spot + half] = piece[row : row + cut, column : column + half].astype(f32)


def out_result(index, pieces, local, width, base):
    cut = local // CHIPS
    return kernel_call(
        functools.partial(out_result_body, local, base),
        shape((local, width), f32),
        [pl.BlockSpec(pieces[0].shape, lambda i, n: (0, 0))] * PIECES,
        pl.BlockSpec((cut, width), lambda i, n: (n[0] ^ i, 0)),
        tuple(pieces),
        index=index,
        grid=(CHIPS,),
        name="out_result",
    )


def lane_sum(value):
    total = value[:, :LANES]
    for n in range(1, value.shape[1] // LANES):
        total = total + value[:, n * LANES : (n + 1) * LANES]
    return total


def feedforward_result_body(ff_local, cut, index, *refs):
    pieces = refs[:CHIPS]
    gate_weight, up_weight, gain = refs[CHIPS : CHIPS + 3]
    gate_out, up_out, gain_out = refs[-3:]
    shards = gate_weight.shape[1] // ff_local
    width = shards * cut
    for chip in range(CHIPS):

        @pl.when(index[0] == chip)
        def _():
            @pl.loop(0, gate_out.shape[0] // 16)
            def _(n):
                rows = pl.ds(pl.multiple_of(n * 16, 16), 16)
                scale = gain[rows, :1]
                total = jnp.zeros((16, LANES), f32)
                for base, weight, out in ((0, gate_weight, gate_out), (width, up_weight, up_out)):
                    parts = []
                    for s in range(shards):
                        for owner in range(CHIPS):
                            start = base + s * cut
                            parts.append(pieces[owner ^ chip][rows, start : start + cut].astype(f32))
                    wide = jnp.concatenate(parts, axis=1)
                    total = total + lane_sum(wide * weight[rows, :].astype(f32))
                    out[rows, :] = wide * scale
                gain_out[rows, :] = total


def feedforward_result(index, side, pieces, gate_weight, up_weight, gain, ff_local, before):
    local, ff = gate_weight.shape
    half = local // 2
    rows = 64
    steps = half // rows
    row = lambda i, n: ((n[1] ^ side) * steps + i, 0)
    in_specs = [pl.BlockSpec((rows, pieces[0].shape[1]), lambda i, n: (i, 0))] * CHIPS
    in_specs += [pl.BlockSpec((rows, ff), row)] * 2 + [pl.BlockSpec((rows, LANES), row)]
    operands = (*pieces, gate_weight, up_weight, gain)
    aliases = {}
    if before is not None:
        aliases = {1 + len(operands) + n: n for n in range(3)}
        in_specs = in_specs + [pl.BlockSpec(memory_space=pl.ANY)] * 3
        operands = operands + tuple(before)
    return kernel_call(
        functools.partial(feedforward_result_body, ff_local, ff_local // CHIPS),
        (shape((local, ff), f32), shape((local, ff), f32), shape((local, LANES), f32)),
        in_specs,
        (pl.BlockSpec((rows, ff), row), pl.BlockSpec((rows, ff), row), pl.BlockSpec((rows, LANES), row)),
        operands,
        index=index,
        grid=(steps,),
        aliases=aliases,
        name="feedforward_result",
    )


def qkv_result_body(local, group_shards, index, *refs):
    pieces = refs[:PIECES]
    weights, gain = refs[PIECES : PIECES + 3], refs[PIECES + 3]
    outs, gain_out = refs[PIECES + 4 : PIECES + 7], refs[PIECES + 7]
    q_width = GROUP * HEAD
    cut = local // CHIPS
    scale = gain[:, :1]
    for chip in range(CHIPS):
        for side in range(2):

            @pl.when((index[0] == chip) & (pl.program_id(0) == side))
            def _():
                parts, k_parts, v_parts = [], [], []
                for group in range(CHIPS):
                    owner = (group >> 1) + 2 * (group & 1)
                    piece = pieces[2 * (owner ^ chip) + side]
                    for s in range(group_shards):
                        for j in range(CHIPS):
                            start = ((j ^ owner) * group_shards + s) * cut
                            parts.append(piece[:, start : start + cut].astype(f32))
                    k_parts.append(piece[:, q_width : q_width + HEAD].astype(f32))
                    v_parts.append(piece[:, q_width + HEAD : q_width + 2 * HEAD].astype(f32))
                total = jnp.zeros((gain.shape[0], LANES), f32)
                for part, weight, out in zip((parts, k_parts, v_parts), weights, outs):
                    wide = jnp.concatenate(part, axis=1)
                    total = total + lane_sum(wide * weight[...].astype(f32))
                    out[...] = wide * scale
                gain_out[...] = total


def qkv_result(index, pieces, query, key, value, gain):
    local, width = query.shape
    half = local // 2
    group_shards = width // local // CHIPS
    row = lambda i, n: (n[1] ^ i, 0)
    kv_width = key.shape[1]
    return kernel_call(
        functools.partial(qkv_result_body, local, group_shards),
        (
            shape((local, width), f32),
            shape((local, kv_width), f32),
            shape((local, kv_width), f32),
            shape((local, LANES), f32),
        ),
        [pl.BlockSpec(pieces[0].shape, lambda i, n: (0, 0))] * PIECES
        + [
            pl.BlockSpec((half, width), row),
            pl.BlockSpec((half, kv_width), row),
            pl.BlockSpec((half, kv_width), row),
            pl.BlockSpec((half, LANES), row),
        ],
        (
            pl.BlockSpec((half, width), row),
            pl.BlockSpec((half, kv_width), row),
            pl.BlockSpec((half, kv_width), row),
            pl.BlockSpec((half, LANES), row),
        ),
        (*pieces, query, key, value, gain),
        index=index,
        grid=(2,),
        name="qkv_result",
    )


def per_device(
    hidden_in,
    attention_gain,
    query_weight,
    key_weight,
    value_weight,
    output_weight,
    feedforward_gain,
    gate_weight,
    up_weight,
    down_weight,
    out_grad,
):
    rows, width = hidden_in.shape
    shards = lax.axis_size("shard")
    replicas = lax.axis_size("replica")
    place = lax.axis_index("replica")
    depth = lax.axis_index("shard")
    core = place & 1
    chip = (place >> 1) & (CHIPS - 1)
    local = width // shards
    half = local // 2
    ff_local = down_weight.shape[0]
    group_shards = shards // CHIPS
    q_width = GROUP * HEAD
    qkv_width = q_width + 2 * HEAD
    index = jnp.stack([chip, core, depth]).astype(jnp.int32)

    gain_one = jnp.broadcast_to(attention_gain.astype(f32)[:, None], (local, LANES))
    gain_two = jnp.broadcast_to(feedforward_gain.astype(f32)[:, None], (local, LANES))


    at_block, out_block = attention_block(
        index, query_weight, key_weight, value_weight, output_weight, gain_one
    )
    x = own_first(index, (after(hidden_in, at_block),), local)[0]
    xs = [x, swap(x, 2)]
    at_own = lax.all_gather(at_block, "shard", axis=0, tiled=True)
    out_all = lax.all_gather(out_block, "shard", axis=0, tiled=True)
    gu_block = feedforward_block(index, gate_weight, up_weight, after(gain_two, at_block), ff_local)
    gu_own = lax.all_gather(gu_block, "shard", axis=0, tiled=True)
    down_own = lax.all_gather(down_block(index, down_weight, local), "shard", axis=0, tiled=True)
    g = own_first(index, (after(out_grad, x),), local)[0]
    g_blocks = [g, swap(g, 2), swap(g, 4)]
    at_own = after(at_own, gu_block, xs[1], *g_blocks[1:])

    qkv_own = [at_own]
    qkv_own.append(swap(qkv_own[0], 4))
    qkv_other = [swap(qkv_own[0], 1)]
    inverse = rope_base ** (-jnp.arange(0, HEAD, 2, dtype=f32) / HEAD)
    places = (depth * rows + jnp.arange(rows, dtype=jnp.int32)).astype(f32)
    angles = inverse[:, None] * places[None, :]
    angles = jnp.concatenate([angles, angles], axis=0)
    cosine, sine = jnp.cos(angles), jnp.sin(angles)

    def shifted(kv):
        return [kv] + [shift(kv, d) for d in range(1, shards)]

    queries, kv, xhat = qkv_call(xs, qkv_own[0], qkv_other[0], cosine, sine)
    kvs = shifted(kv)
    qkv_own[1] = after(qkv_own[1], *kvs[1:])
    qkv_other.append(swap(qkv_own[1], 1))
    queries_two, kv_two = qkv_call(xhat, qkv_own[1], qkv_other[1], cosine, sine)
    kvs_two = shifted(kv_two)
    groups = [(queries, *attention_call(index, queries, kvs), kvs)]
    groups.append((queries_two, *attention_call(index, queries_two, kvs_two), kvs_two))
    attended = [group[2] for group in groups]
    groups = [(group[0], group[1], group[3], group[4]) for group in groups]

    out_all = after(out_all, qkv_own[1])
    x_place = chip & 1
    low_group = (chip >> 1) == 0
    pair_rows = PAIR * group_shards * half // 2

    def out_for(mask):
        return lax.dynamic_slice_in_dim(out_all, ((chip ^ mask) & 1) * pair_rows, pair_rows, 0)

    out_pieces = [out_for(0)] + [swap(out_for(m), 2 * m) for m in range(1, CHIPS)]
    wo_own = out_rows_call(index, [after(piece, *kvs_two[1:]) for piece in out_pieces])
    wo_other = swap(wo_own, 1)

    mid_terms = [(attended[n], wo_own, wo_other, n) for n in range(PAIR)]
    g_blocks.append(swap(after(g, *out_pieces[1:]), 6))
    mid_out = parts_call(mid_terms, rows, False, "attention_out")
    g_all = jnp.concatenate([after(block, mid_out[0]) for block in g_blocks], axis=0)
    middle, two = middle_call(plane_send(mid_out), after(x, g_all))
    twos = plane_gather_forward(two)

    gu_own = after(gu_own, *twos[1:])
    gu_other = swap(gu_own, 1)
    act, for_gate, for_up, two_all = gate_call(twos, gu_own, gu_other)

    def over_groups(kept):
        if replicas > PIECES:
            groups = [
                [e * PIECES + i for e in range(replicas // PIECES)] for i in range(PIECES)
            ]
            kept = lax.psum(kept, "replica", axis_index_groups=groups)
        return kept

    def reduced(term):
        kept = lax.psum_scatter(term, "shard", scatter_dimension=0, tiled=True)
        return over_groups(kept)

    def plane_pieces(kept):
        mine = plane_gather(kept)
        return mine, [swap(part, 1) for part in mine]

    def mixed(mine, theirs):
        return [part for pair in zip(mine, theirs) for part in pair]

    down_sent = weight_grad(act, None, g_all, 1, width // 2, 1, (), "down_grad_other")
    down_sent = [swap(down_sent[0], 1)]
    down_sent[0] = after(down_sent[0], down_own)
    down_term = weight_grad(act, None, g_all, 0, width // 2, 1, (down_sent,), "down_grad")[0]
    down_kept = reduced(down_term)
    down_other = swap(down_own, 1)

    grads = hidden_back_call(after(g_all, down_term), down_own, down_other, for_gate, for_up)
    grads_wide = grads.shape[1]
    gu_sent = weight_grad(two_all, 1, grads, 0, grads_wide, 1, (), "gate_grad_other")
    gu_sent = [swap(gu_sent[0], 1)]
    gu_term = weight_grad(two_all, 0, grads, 0, grads_wide, 1, (gu_sent,), "gate_grad")[0]
    gu_kept = reduced(gu_term)
    grads_late = after(grads, gu_term)
    e_terms = parts_call([(grads_late, gu_own, gu_other, 0)], rows, True, "feedforward_back")
    e_parts = plane_send(e_terms)
    act_late = after(act, e_terms[0])
    out_terms = parts_call([(act_late, down_own, down_other, 0)], rows, False, "feedforward_out")

    middle_late = after(middle, out_terms[0], down_kept)
    grad_middle, branch = grad_middle_call(e_parts, middle_late, g)
    branches = [branch, swap(branch, 2)]

    def back_block(m, block, before):
        return attention_back_call(index, m, block, wo_own, wo_other, cosine, sine, groups, before)

    before = back_block(0, branch, None)
    out_parts = plane_send(after(out_terms, branches[1], before[1]))
    before = back_block(1, after(branches[1], before[1]), before)
    output = output_call(index, out_parts, middle, local)
    grad_q, grad_first, grad_rest = before
    grad_rest = after(grad_rest, *out_parts[1:3])
    rest = [shift(grad_rest[d - 1], -d) for d in range(1, shards)]

    half_wide = width // 2
    branch_all = jnp.concatenate([after(block, grad_first, *out_parts[1:3]) for block in branches], axis=0)
    both_attended = jnp.concatenate(attended, axis=1)
    wo_sent = weight_grad(both_attended, None, branch_all, 1, half_wide, 1, (), "out_grad_other")
    wo_sent = [after(swap(wo_sent[0], 1), rest[-1])]
    wo_term = weight_grad(both_attended, None, branch_all, 0, half_wide, 1, (wo_sent,), "out_grad")[0]
    wo_terms = out_sends(index, wo_term)
    wo_parts = plane_send(wo_terms)
    wo_wide = out_block_call(index, [after(wo_parts[0], gu_kept), *wo_parts[1:]], shards)
    grad_first = after(grad_first, out_parts[3], wo_terms[0])
    grad_qkv = grad_qkv_call(grad_q, grad_first, rest, cosine, sine)

    def qkv_grad(n, side, added, name):
        return weight_grad(xhat, side, grad_qkv[n], 0, qkv_width, 1, added, name)

    qkv_sent = [swap(qkv_grad(n, 1, (), "qkv_grad_other")[0], 1) for n in (1, 0)]
    back_terms = [(grad_qkv[n], qkv_own[n], qkv_other[n], 0) for n in range(PAIR)]
    qkv_sent[0] = after(qkv_sent[0], *wo_parts[1:3])
    qkv_second = qkv_grad(1, 0, ([qkv_sent[0]],), "qkv_grad")[0]
    qkv_term = qkv_grad(0, 0, ([qkv_sent[1]],), "qkv_grad")[0]
    at_term = jnp.concatenate([qkv_term, qkv_second, wo_wide], axis=1)
    at_kept = reduced(after(at_term, gu_kept))
    back_terms[0] = (after(grad_qkv[0], qkv_term, qkv_second), *back_terms[0][1:])
    back_parts = parts_call(back_terms, rows, True, "qkv_back")
    e_one = plane_send(back_parts)
    gu_mine = plane_gather_forward(gu_kept, back_parts[0])
    gu_mine = gu_mine[:3] + [jnp.concatenate(gu_mine[3:], axis=0)]
    gu_theirs = [swap(after(part, output), 1) for part in gu_mine]
    gu_out = feedforward_result(index, 0, gu_mine, gate_weight, up_weight, gain_two, ff_local, None)
    at_kept = after(at_kept, gu_out[0])
    gu_out = feedforward_result(index, 1, gu_theirs, gate_weight, up_weight, gain_two, ff_local, gu_out)

    down_mine = plane_gather(after(down_kept, *gu_mine[1:]))
    down_theirs = [swap(part, 1) for part in down_mine]
    down_out = rows_result(index, mixed(down_mine, down_theirs), local, "down_result")
    grad_input = grad_input_call(index, e_one, x, grad_middle, local)

    second = swap(at_kept[:, qkv_width : 2 * qkv_width], 4)
    first = at_kept[:, :qkv_width].astype(f32) + second.astype(f32)
    at_kept = jnp.concatenate([first.astype(bf16), at_kept[:, 2 * qkv_width :]], axis=1)
    at_pieces = mixed(*plane_pieces(at_kept))
    at_pieces[0] = after(at_pieces[0], gu_out[0], down_out, grad_input)
    wo_out = out_result(index, at_pieces, local, width, qkv_width)
    q_out, k_out, v_out, gain_one_sums = qkv_result(
        index, at_pieces, query_weight, key_weight, value_weight, gain_one
    )
    return (
        output,
        grad_input,
        jnp.sum(gain_one_sums, axis=1),
        q_out,
        k_out,
        v_out,
        wo_out,
        jnp.sum(gu_out[2], axis=1),
        gu_out[0],
        gu_out[1],
        down_out,
    )


def solution(mesh):
    return jax.shard_map(
        per_device,
        mesh=mesh,
        in_specs=(
            P(("replica", "shard"), None),
            P("shard"),
            P("shard", None),
            P("shard", None),
            P("shard", None),
            P("shard", None),
            P("shard"),
            P("shard", None),
            P("shard", None),
            P("shard", None),
            P(("replica", "shard"), None),
        ),
        out_specs=(
            P(("replica", "shard"), None),
            P(("replica", "shard"), None),
            P("shard"),
            P("shard", None),
            P("shard", None),
            P("shard", None),
            P("shard", None),
            P("shard"),
            P("shard", None),
            P("shard", None),
            P("shard", None),
        ),
        check_vma=False,
    )
```

profile of v0, /device:TPU:0, one launch (start us, length us, event | category | flops | bytes accessed | tf_op | source)
XLA Modules:
  0.0 696.3 jit_solution(10012511646175827580)
XLA Ops:
  13.9 5.2 feedforward_block.1
  25.5 15.7 %collective-permute-done.refs_1_ = bf16[192,2048]{1,0:T(8,128)(2,1)S(1)} collective-permute-done((bf16[192,2048]{1,0:T(8,128)(2,1)S(1)}, bf16[192,2048]{1,0:T(8,128)(2,1)S(1)}, u32[]{:S(2)}, u32[]{:S(2)}) %collective-permute-start) | collective-permute-done | bytes 786464 | tf_op jit(solution)/shard_map/ppermute | solution.py:79
  41.2 16.0 %collective-permute-done.1 = bf16[192,2048]{1,0:T(8,128)(2,1)S(1)} collective-permute-done((bf16[192,2048]{1,0:T(8,128)(2,1)S(1)}, bf16[192,2048]{1,0:T(8,128)(2,1)S(1)}, u32[]{:S(2)}, u32[]{:S(2)}) %collective-permute-start.1) | collective-permute-done | bytes 786464 | tf_op jit(solution)/shard_map/ppermute | solution.py:79
  70.1 4.5 collective-permute-start.5
  75.9 13.6 %collective-permute-done.7.refs_1_.refs_3_ = bf16[1024,640]{1,0:T(8,128)(2,1)S(1)} collective-permute-done((bf16[1024,640]{1,0:T(8,128)(2,1)}, bf16[1024,640]{1,0:T(8,128)(2,1)S(1)}, u32[]{:S(2)}, u32[]{:S(2)}) %collective-permute-start.7) | collective-permute-done | bytes 1310752 | tf_op jit(solution)/shard_map/ppermute | solution.py:79
  103.7 4.5 collective-permute-start.10
  108.8 7.3 %collective-permute-start.11 = (bf16[384,128]{1,0:T(8,128)(2,1)S(1)}, bf16[384,128]{1,0:T(8,128)(2,1)S(1)}, u32[]{:S(2)}, u32[]{:S(2)}) collective-permute-start(bf16[384,128]{1,0:T(8,128)(2,1)S(1)} %get-tuple-element.122.refs_0_.refs_10_), channel_id=1, source_target_pairs={{0,3},{4,7},{8,11},{12,15},{16,19},{20,23},{24,27},{28,31}} | collective-permute-start | bytes 294920 | tf_op jit(solution)/shard_map/ppermute | solution.py:85
  116.2 4.6 collective-permute-done.11.refs_3_.refs_13_
  127.1 4.5 attention.2
  131.6 4.5 attention.3
  138.3 7.4 %attention_out.1 = (f32[192,2048]{1,0:T(8,128)}, bf16[192,2048]{1,0:T(8,128)(2,1)S(1)}) custom-call(bf16[384,512]{1,0:T(8,128)(2,1)S(1)} %get-tuple-element.118.refs_0_, bf16[384,512]{1,0:T(8,128)(2,1)S(1)} %get-tuple-element.123.refs_1_, bf16[1024,1024]{1,0:T(8,128)(2,1)} %out_rows.1.refs_2_.refs_3_.wo_own, ...), custom_call_target="tpu_custom_call" | custom-call | tf_op jit(solution)/shard_map/attention_out/pallas_call | solution.py:69
  148.2 17.2 %collective-permute-done.16.refs_1_ = bf16[192,2048]{1,0:T(8,128)(2,1)S(1)} collective-permute-done((bf16[192,2048]{1,0:T(8,128)(2,1)S(1)}, bf16[192,2048]{1,0:T(8,128)(2,1)S(1)}, u32[]{:S(2)}, u32[]{:S(2)}) %collective-permute-start.16) | collective-permute-done | bytes 786464 | tf_op jit(solution)/shard_map/ppermute | solution.py:79
  169.7 17.7 %collective-permute-done.18.refs_1_ = bf16[192,2048]{1,0:T(8,128)(2,1)S(1)} collective-permute-done((bf16[192,2048]{1,0:T(8,128)(2,1)S(1)}, bf16[192,2048]{1,0:T(8,128)(2,1)S(1)}, u32[]{:S(2)}, u32[]{:S(2)}) %collective-permute-start.18) | collective-permute-done | bytes 786464 | tf_op jit(solution)/shard_map/ppermute | solution.py:79
  202.8 6.6 collective-permute-done.22.refs_7_.refs_8_.refs_2_
  209.4 17.1 %gate.3 = (bf16[768,1408]{1,0:T(8,128)(2,1)}, bf16[768,1408]{1,0:T(8,128)(2,1)}, bf16[768,1408]{1,0:T(8,128)(2,1)}, bf16[768,2048]{1,0:T(8,128)(2,1)}) custom-call(bf16[192,2048]{1,0:T(8,128)(2,1)S(1)} %get-tuple-element.138.refs_0_, bf16[192,2048]{1,0:T(8,128)(2,1)} %copy-done.56, bf16[192,2048]{1,0:T(8,128)(2,1)} %copy-done.57, ...), custom_call_target="tpu_custom_call" | custom-call | tf_op jit(solution)/shard_map/gate/pallas_call | solution.py:69
  226.5 6.8 down_grad_other.1
  233.5 32.3 %all-gather.11.cloned.1.call-done.own.refs_1_ = bf16[1408,1024]{1,0:T(8,128)(2,1)} async-done(((bf16[352,1024]{1,0:T(8,128)(2,1)}), bf16[1408,1024]{1,0:T(8,128)(2,1)}) %all-gather.11.cloned.1.call-update) | async-done | bytes 2883600 | tf_op jit(solution)/shard_map/all_gather | solution.py:1125
  265.8 7.3 %down_grad.1 = bf16[1408,1024]{1,0:T(8,128)(2,1)} custom-call(bf16[768,1408]{1,0:T(8,128)(2,1)} %get-tuple-element.148.left.refs_0_, bf16[768,2048]{1,0:T(8,128)(2,1)} %copy-done.51, bf16[1408,1024]{1,0:T(8,128)(2,1)} %collective-permute-done.23.refs_0_), custom_call_target="tpu_custom_call" | custom-call | tf_op jit(solution)/shard_map/down_grad/pallas_call | solution.py:69
  273.1 10.9 %hidden_back.1.right.refs_0_ = bf16[768,2816]{1,0:T(8,128)(2,1)} custom-call(bf16[768,2048]{1,0:T(8,128)(2,1)} %copy-done.51, bf16[1408,1024]{1,0:T(8,128)(2,1)} %all-gather.11.cloned.1.call-done.own.refs_1_, bf16[1408,1024]{1,0:T(8,128)(2,1)} %collective-permute-done.24.other.refs_2_, bf16[768,1408]{1,0:T(8,128)(2,1)} %get-tuple-element.143.for_gate, ...), custom_call_target="tpu_custom_call" | custom-call | tf_op jit(solution)/shard_map/hidden_back/pallas_call | solution.py:69
  284.1 12.3 %gate_grad_other.1 = bf16[1024,2816]{1,0:T(8,128)(2,1)} custom-call(bf16[768,2048]{1,0:T(8,128)(2,1)} %get-tuple-element.145.left, bf16[768,2816]{1,0:T(8,128)(2,1)} %hidden_back.1.right.refs_0_), custom_call_target="tpu_custom_call" | custom-call | tf_op jit(solution)/shard_map/gate_grad_other/pallas_call | solution.py:69
  297.0 9.3 %collective-permute-done.25.refs_0_ = bf16[1024,2816]{1,0:T(8,128)(2,1)} collective-permute-done((bf16[1024,2816]{1,0:T(8,128)(2,1)}, bf16[1024,2816]{1,0:T(8,128)(2,1)}, u32[]{:S(2)}, u32[]{:S(2)}) %collective-permute-start.25) | collective-permute-done | bytes 5767200 | tf_op jit(solution)/shard_map/ppermute | solution.py:79
  306.3 13.4 %gate_grad.1 = bf16[1024,2816]{1,0:T(8,128)(2,1)} custom-call(bf16[768,2048]{1,0:T(8,128)(2,1)} %get-tuple-element.145.left, bf16[768,2816]{1,0:T(8,128)(2,1)} %hidden_back.1.right.refs_0_, bf16[1024,2816]{1,0:T(8,128)(2,1)} %collective-permute-done.25.refs_0_), custom_call_target="tpu_custom_call" | custom-call | tf_op jit(solution)/shard_map/gate_grad/pallas_call | solution.py:69
  319.8 15.4 %feedforward_back.1 = (f32[192,2048]{1,0:T(8,128)}, bf16[192,2048]{1,0:T(8,128)(2,1)}, bf16[192,2048]{1,0:T(8,128)(2,1)}, bf16[192,2048]{1,0:T(8,128)(2,1)}) custom-call(bf16[768,2816]{1,0:T(8,128)(2,1)} %hidden_back.1.right.refs_0_, bf16[1024,2816]{1,0:T(8,128)(2,1)} %all-gather.9.cloned.1.call-done.refs_5_.refs_6_.refs_1_, ...), custom_call_target="tpu_custom_call" | custom-call | tf_op jit(solution)/shard_map/feedforward_back/pallas_call | solution.py:69
  338.7 11.0 %feedforward_out.1 = (f32[192,2048]{1,0:T(8,128)}, bf16[192,2048]{1,0:T(8,128)(2,1)S(1)}, bf16[192,2048]{1,0:T(8,128)(2,1)S(1)}, bf16[192,2048]{1,0:T(8,128)(2,1)}) custom-call(bf16[768,1408]{1,0:T(8,128)(2,1)} %get-tuple-element.148.left.refs_0_, bf16[1408,1024]{1,0:T(8,128)(2,1)} %all-gather.11.cloned.1.call-done.own.refs_1_, ...), custom_call_target="tpu_custom_call" | custom-call | tf_op jit(solution)/shard_map/feedforward_out/pallas_call | solution.py:69
  356.6 16.8 %collective-permute-done.27.refs_2_ = bf16[192,2048]{1,0:T(8,128)(2,1)} collective-permute-done((bf16[192,2048]{1,0:T(8,128)(2,1)}, bf16[192,2048]{1,0:T(8,128)(2,1)}, u32[]{:S(2)}, u32[]{:S(2)}) %collective-permute-start.27) | collective-permute-done | bytes 786464 | tf_op jit(solution)/shard_map/ppermute | solution.py:79
  374.6 4.8 grad_middle.1
  385.2 13.2 %attention_back.2 = (bf16[384,1024]{1,0:T(8,128)(2,1)}, f32[384,256]{1,0:T(8,128)S(1)}, bf16[3,384,256]{2,1,0:T(8,128)(2,1)}) custom-call(s32[3]{0:T(128)S(1)} %pad_add_fusion.index, bf16[192,2048]{1,0:T(8,128)(2,1)} %copy-done.9, bf16[1024,1024]{1,0:T(8,128)(2,1)} %out_rows.1.refs_2_.refs_3_.wo_own, bf16[1024,1024]{1,0:T(8,128)(2,1)} %copy-done.50, ...), custom_call_target="tpu_custom_call" | custom-call | bytes 47970000 | tf_op jit(solution)/shard_map/attention_back/pallas_call | solution.py:74
  400.9 13.3 %attention_back.3 = (bf16[384,1024]{1,0:T(8,128)(2,1)}, f32[384,256]{1,0:T(8,128)S(1)}, bf16[3,384,256]{2,1,0:T(8,128)(2,1)}) custom-call(s32[3]{0:T(128)S(1)} %pad_add_fusion.index, bf16[192,2048]{1,0:T(8,128)(2,1)} %collective-permute-done.29.branch, ...), custom_call_target="tpu_custom_call", output_to_operand_aliasing={{0}: (20, {}), {1}: (21, {}), {2}: (22, {})} | custom-call | bytes 47970000 | tf_op jit(solution)/shard_map/attention_back/pallas_call | solution.py:74
  420.3 4.7 out_grad_other.1
  430.4 11.8 %collective-permute-done.34.refs_2_ = bf16[384,256]{1,0:T(8,128)(2,1)S(1)} collective-permute-done((bf16[384,256]{1,0:T(8,128)(2,1)S(1)}, bf16[384,256]{1,0:T(8,128)(2,1)S(1)}, u32[]{:S(2)}, u32[]{:S(2)}) %collective-permute-start.34) | collective-permute-done | bytes 196640 | tf_op jit(solution)/shard_map/ppermute | solution.py:85
  443.5 5.0 out_grad.1.term
  452.4 16.1 %collective-permute-done.36.refs_1_ = bf16[384,256]{1,0:T(8,128)(2,1)S(1)} collective-permute-done((bf16[384,256]{1,0:T(8,128)(2,1)S(1)}, bf16[384,256]{1,0:T(8,128)(2,1)S(1)}, u32[]{:S(2)}, u32[]{:S(2)}) %collective-permute-start.36) | collective-permute-done | bytes 196640 | tf_op jit(solution)/shard_map/ppermute | solution.py:85
  480.3 11.3 %collective-permute-done.39.refs_1_ = bf16[256,1024]{1,0:T(8,128)(2,1)S(1)} collective-permute-done((bf16[256,1024]{1,0:T(8,128)(2,1)S(1)}, bf16[256,1024]{1,0:T(8,128)(2,1)S(1)}, u32[]{:S(2)}, u32[]{:S(2)}) %collective-permute-start.39) | collective-permute-done | bytes 524320 | tf_op jit(solution)/shard_map/ppermute | solution.py:79
  491.6 11.5 %collective-permute-done.40.refs_2_ = bf16[256,1024]{1,0:T(8,128)(2,1)S(1)} collective-permute-done((bf16[256,1024]{1,0:T(8,128)(2,1)S(1)}, bf16[256,1024]{1,0:T(8,128)(2,1)S(1)}, u32[]{:S(2)}, u32[]{:S(2)}) %collective-permute-start.40) | collective-permute-done | bytes 524320 | tf_op jit(solution)/shard_map/ppermute | solution.py:79
  523.1 8.2 %qkv_back.1 = (f32[192,2048]{1,0:T(8,128)}, bf16[192,2048]{1,0:T(8,128)(2,1)S(1)}) custom-call(bf16[384,640]{1,0:T(8,128)(2,1)S(1)} %get-tuple-element.185.right.refs_0_, bf16[384,640]{1,0:T(8,128)(2,1)S(1)} %copy-done.5, bf16[1024,640]{1,0:T(8,128)(2,1)} %all-gather.5.cloned.1.call-done.refs_2_, bf16[1024,640]{1,0:T(8,128)(2,1)} %copy-done.3, ...), custom_call_target="tpu_custom_call" | custom-call | tf_op jit(solution)/shard_map/qkv_back/pallas_call | solution.py:69
  531.3 18.9 %collective-permute-done.43.refs_1_ = bf16[256,2816]{1,0:T(8,128)(2,1)} collective-permute-done((bf16[256,2816]{1,0:T(8,128)(2,1)S(1)}, bf16[256,2816]{1,0:T(8,128)(2,1)}, u32[]{:S(2)}, u32[]{:S(2)}) %collective-permute-start.43) | collective-permute-done | bytes 1441824 | tf_op jit(solution)/shard_map/ppermute | solution.py:79
  555.4 4.4 output.1
  562.8 4.8 collective-permute-done.46
  570.2 14.2 %collective-permute-done.41.refs_1_ = bf16[192,2048]{1,0:T(8,128)(2,1)S(1)} collective-permute-done((bf16[192,2048]{1,0:T(8,128)(2,1)S(1)}, bf16[192,2048]{1,0:T(8,128)(2,1)S(1)}, u32[]{:S(2)}, u32[]{:S(2)}) %collective-permute-start.41) | collective-permute-done | bytes 786464 | tf_op jit(solution)/shard_map/ppermute | solution.py:79
  589.6 10.2 %feedforward_result.2 = (f32[512,5632]{1,0:T(8,128)}, f32[512,5632]{1,0:T(8,128)}, f32[512,128]{1,0:T(8,128)S(1)}) custom-call(s32[3]{0:T(128)S(1)} %pad_add_fusion.index, bf16[256,2816]{1,0:T(8,128)(2,1)S(1)} %copy-done.19, bf16[256,2816]{1,0:T(8,128)(2,1)} %collective-permute-done.43.refs_1_, bf16[256,2816]{1,0:T(8,128)(2,1)} %collective-permute-done.44.refs_2_, ...), custom_call_target="tpu_custom_call" | custom-call | tf_op jit(solution)/shard_map/feedforward_result/pallas_call | solution.py:74
  601.6 14.4 %collective-permute-done.55.refs_4_ = bf16[352,1024]{1,0:T(8,128)(2,1)} collective-permute-done((bf16[352,1024]{1,0:T(8,128)(2,1)}, bf16[352,1024]{1,0:T(8,128)(2,1)}, u32[]{:S(2)}, u32[]{:S(2)}) %collective-permute-start.55) | collective-permute-done | bytes 720928 | tf_op jit(solution)/shard_map/ppermute | solution.py:79
  616.0 4.8 collective-permute-done.47
  626.1 12.8 %collective-permute-done.60.refs_2_ = bf16[256,1152]{1,0:T(8,128)(2,1)} collective-permute-done((bf16[256,1152]{1,0:T(8,128)(2,1)S(1)}, bf16[256,1152]{1,0:T(8,128)(2,1)}, u32[]{:S(2)}, u32[]{:S(2)}) %collective-permute-start.60) | collective-permute-done | bytes 589856 | tf_op jit(solution)/shard_map/ppermute | solution.py:79
  638.9 12.1 %collective-permute-done.62.refs_4_ = bf16[256,1152]{1,0:T(8,128)(2,1)} collective-permute-done((bf16[256,1152]{1,0:T(8,128)(2,1)S(1)}, bf16[256,1152]{1,0:T(8,128)(2,1)}, u32[]{:S(2)}, u32[]{:S(2)}) %collective-permute-start.62) | collective-permute-done | bytes 589856 | tf_op jit(solution)/shard_map/ppermute | solution.py:79
  655.6 7.9 %down_result.1 = f32[1408,2048]{1,0:T(8,128)} custom-call(s32[3]{0:T(128)S(1)} %pad_add_fusion.index, bf16[352,1024]{1,0:T(8,128)(2,1)} %reduce-scatter.4.cloned.1.call-done.refs_0_, bf16[352,1024]{1,0:T(8,128)(2,1)S(1)} %collective-permute-done.52.refs_1_, bf16[352,1024]{1,0:T(8,128)(2,1)} %collective-permute-done.53.refs_2_, bf16[352,1024]{1,0:T(8,128)(2,1)} %copy-done.65, ...), custom_call_target="tpu_custom_call" | custom-call | tf_op jit(solution)/shard_map/down_result/pallas_call | solution.py:74
  664.6 10.2 %feedforward_result.3 = (f32[512,5632]{1,0:T(8,128)}, f32[512,5632]{1,0:T(8,128)}, f32[512,128]{1,0:T(8,128)S(1)}) custom-call(s32[3]{0:T(128)S(1)} %pad_add_fusion.index, bf16[256,2816]{1,0:T(8,128)(2,1)S(1)} %copy-done.18, bf16[256,2816]{1,0:T(8,128)(2,1)} %collective-permute-done.49.refs_1_, ...), custom_call_target="tpu_custom_call", output_to_operand_aliasing={{0}: (8, {}), {1}: (9, {}), {2}: (10, {})} | custom-call | tf_op jit(solution)/shard_map/feedforward_result/pallas_call | solution.py:74
  676.4 6.0 qkv_result.1
  684.2 5.0 out_result.1
  (322 shorter events, 173.4 us)
Async XLA Ops:
  7.2 50.1 %all-gather.5.cloned.1.call-start = ((), (), s32[]{:S(2)}) async-start(), calls=%async_computation.3 | async-start | bytes 1638400 | tf_op jit(solution)/shard_map/all_gather | solution.py:1121
  13.0 77.9 %all-gather.7.cloned.1.call-start = ((), (), s32[]{:S(2)}) async-start(), calls=%async_computation.4 | async-start | bytes 1310720 | tf_op jit(solution)/shard_map/all_gather | solution.py:1122
  13.7 180.7 %all-gather.9.cloned.1.call-start = ((), (), s32[]{:S(2)}) async-start(), calls=%async_computation.5 | async-start | bytes 7208960 | tf_op jit(solution)/shard_map/all_gather | solution.py:1124
  19.1 246.7 %all-gather.11.cloned.1.call-start = ((), (), s32[]{:S(2)}) async-start(), calls=%async_computation.6 | async-start | bytes 3604480 | tf_op jit(solution)/shard_map/all_gather | solution.py:1125
  19.8 21.4 %collective-permute-start = (bf16[192,2048]{1,0:T(8,128)(2,1)S(1)}, bf16[192,2048]{1,0:T(8,128)(2,1)S(1)}, u32[]{:S(2)}, u32[]{:S(2)}) collective-permute-start(bf16[192,2048]{1,0:T(8,128)(2,1)S(1)} %own_first.2.refs_0_.refs_2_), channel_id=1, source_target_pairs={{0,8},{4,12},{8,0},{12,4},{16,24},{20,28},{24,16},{28,20},{1,9},{5... | collective-permute-start | bytes 2359304 | tf_op jit(solution)/shard_map/ppermute | solution.py:79
  23.4 33.8 %collective-permute-start.1 = (bf16[192,2048]{1,0:T(8,128)(2,1)S(1)}, bf16[192,2048]{1,0:T(8,128)(2,1)S(1)}, u32[]{:S(2)}, u32[]{:S(2)}) collective-permute-start(bf16[192,2048]{1,0:T(8,128)(2,1)S(1)} %own_first.3.refs_5_), channel_id=1, source_target_pairs={{0,8},{4,12},{8,0},{12,4},{16,24},{20,28},{24,16},{28,20},{1,9},{5... | collective-permute-start | bytes 2359304 | tf_op jit(solution)/shard_map/ppermute | solution.py:79
  23.9 33.4 %collective-permute-start.2 = (bf16[192,2048]{1,0:T(8,128)(2,1)S(1)}, bf16[192,2048]{1,0:T(8,128)(2,1)}, u32[]{:S(2)}, u32[]{:S(2)}) collective-permute-start(bf16[192,2048]{1,0:T(8,128)(2,1)S(1)} %own_first.3.refs_5_), channel_id=1, source_target_pairs={{0,16},{4,20},{8,24},{12,28},{16,0},{20,4},{24,8},{28,12},{1,17},{... | collective-permute-start | bytes 2359304 | tf_op jit(solution)/shard_map/ppermute | solution.py:79
  58.1 31.4 %collective-permute-start.7 = (bf16[1024,640]{1,0:T(8,128)(2,1)}, bf16[1024,640]{1,0:T(8,128)(2,1)S(1)}, u32[]{:S(2)}, u32[]{:S(2)}) collective-permute-start(bf16[1024,640]{1,0:T(8,128)(2,1)} %all-gather.5.cloned.1.call-done.refs_2_), channel_id=1, source_target_pairs={{0,16},{4,20},{8,24},{12,28},{16,0},{20,4},{24,8},{28,12},{1,17},{... | collective-permute-start | bytes 3932168 | tf_op jit(solution)/shard_map/ppermute | solution.py:79
  66.3 23.2 %collective-permute-start.4 = (bf16[384,128]{1,0:T(8,128)(2,1)S(1)}, bf16[384,128]{1,0:T(8,128)(2,1)S(1)}, u32[]{:S(2)}, u32[]{:S(2)}) collective-permute-start(bf16[384,128]{1,0:T(8,128)(2,1)S(1)} %get-tuple-element.117.refs_0_.refs_3_), channel_id=1, source_target_pairs={{0,1},{1,2},{2,3},{4,5},{5,6},{6,7},{8,9},{9,10},{10,11},{12,13},{... | collective-permute-start | bytes 294920 | tf_op jit(solution)/shard_map/ppermute | solution.py:85
  92.7 28.0 %collective-permute-start.12 = (bf16[256,1024]{1,0:T(8,128)(2,1)S(1)}, bf16[256,1024]{1,0:T(8,128)(2,1)S(1)}, u32[]{:S(2)}, u32[]{:S(2)}) collective-permute-start(bf16[256,1024]{1,0:T(8,128)(2,1)S(1)} %get-tuple-element.213), channel_id=1, source_target_pairs={{0,8},{4,12},{8,0},{12,4},{16,24},{20,28},{24,16},{28,20},{1,9},{5... | collective-permute-start | bytes 1572872 | tf_op jit(solution)/shard_map/ppermute | solution.py:79
  94.5 26.3 %collective-permute-start.13 = (bf16[256,1024]{1,0:T(8,128)(2,1)S(1)}, bf16[256,1024]{1,0:T(8,128)(2,1)S(1)}, u32[]{:S(2)}, u32[]{:S(2)}) collective-permute-start(bf16[256,1024]{1,0:T(8,128)(2,1)S(1)} %get-tuple-element.212), channel_id=1, source_target_pairs={{0,16},{4,20},{8,24},{12,28},{16,0},{20,4},{24,8},{28,12},{1,17},{... | collective-permute-start | bytes 1572872 | tf_op jit(solution)/shard_map/ppermute | solution.py:79
  95.9 24.9 %collective-permute-start.14 = (bf16[256,1024]{1,0:T(8,128)(2,1)S(1)}, bf16[256,1024]{1,0:T(8,128)(2,1)S(1)}, u32[]{:S(2)}, u32[]{:S(2)}) collective-permute-start(bf16[256,1024]{1,0:T(8,128)(2,1)S(1)} %get-tuple-element.211), channel_id=1, source_target_pairs={{0,24},{4,28},{8,16},{12,20},{16,8},{20,12},{24,0},{28,4},{1,25},{... | collective-permute-start | bytes 1572872 | tf_op jit(solution)/shard_map/ppermute | solution.py:79
  124.8 21.6 %collective-permute-start.17 = (bf16[192,2048]{1,0:T(8,128)(2,1)S(1)}, bf16[192,2048]{1,0:T(8,128)(2,1)S(1)}, u32[]{:S(2)}, u32[]{:S(2)}) collective-permute-start(bf16[192,2048]{1,0:T(8,128)(2,1)S(1)} %own_first.3.refs_5_), channel_id=1, source_target_pairs={{0,24},{4,28},{8,16},{12,20},{16,8},{20,12},{24,0},{28,4},{1,25},{... | collective-permute-start | bytes 2359304 | tf_op jit(solution)/shard_map/ppermute | solution.py:79
  145.7 19.7 %collective-permute-start.16 = (bf16[192,2048]{1,0:T(8,128)(2,1)S(1)}, bf16[192,2048]{1,0:T(8,128)(2,1)S(1)}, u32[]{:S(2)}, u32[]{:S(2)}) collective-permute-start(bf16[192,2048]{1,0:T(8,128)(2,1)S(1)} %get-tuple-element.131), channel_id=1, source_target_pairs={{0,8},{4,12},{8,0},{12,4},{16,24},{20,28},{24,16},{28,20},{1,9},{5... | collective-permute-start | bytes 2359304 | tf_op jit(solution)/shard_map/ppermute | solution.py:79
  169.1 19.8 %collective-permute-start.19 = (bf16[192,2048]{1,0:T(8,128)(2,1)S(1)}, bf16[192,2048]{1,0:T(8,128)(2,1)S(1)}, u32[]{:S(2)}, u32[]{:S(2)}) collective-permute-start(bf16[192,2048]{1,0:T(8,128)(2,1)S(1)} %get-tuple-element.138.refs_0_), channel_id=1, source_target_pairs={{0,16},{4,20},{8,24},{12,28},{16,0},{20,4},{24,8},{28,12},{1,17},{... | collective-permute-start | bytes 2359304 | tf_op jit(solution)/shard_map/ppermute | solution.py:79
  202.5 149.4 %reduce-scatter.4.cloned.1.call-start = ((), (), s32[]{:S(2)}) async-start(), calls=%async_computation.7 | async-start | bytes 3604480 | tf_op jit(solution)/shard_map/reduce_scatter | solution.py:1185
  233.3 32.5 %collective-permute-start.23 = (bf16[1408,1024]{1,0:T(8,128)(2,1)}, bf16[1408,1024]{1,0:T(8,128)(2,1)}, u32[]{:S(2)}, u32[]{:S(2)}) collective-permute-start(bf16[1408,1024]{1,0:T(8,128)(2,1)} %down_grad_other.1), channel_id=1, source_target_pairs={{0,4},{4,0},{8,12},{12,8},{16,20},{20,16},{24,28},{28,24},{1,5},{5... | collective-permute-start | bytes 8650760 | tf_op jit(solution)/shard_map/ppermute | solution.py:79
  296.9 213.4 %reduce-scatter.6.cloned.1.call-start = ((), (), s32[]{:S(2)}) async-start(), calls=%async_computation.8 | async-start | bytes 7208960 | tf_op jit(solution)/shard_map/reduce_scatter | solution.py:1185
  319.8 280.1 %reduce-scatter.8.cloned.1.call-start = ((), (), s32[]{:S(2)}) async-start(), calls=%async_computation.9 | async-start | bytes 4587520 | tf_op jit(solution)/shard_map/reduce_scatter | solution.py:1185
  335.2 20.6 %collective-permute-start.26 = (bf16[192,2048]{1,0:T(8,128)(2,1)}, bf16[192,2048]{1,0:T(8,128)(2,1)S(1)}, u32[]{:S(2)}, u32[]{:S(2)}) collective-permute-start(bf16[192,2048]{1,0:T(8,128)(2,1)} %get-tuple-element.153), channel_id=1, source_target_pairs={{0,8},{4,12},{8,0},{12,4},{16,24},{20,28},{24,16},{28,20},{1,9},{5... | collective-permute-start | bytes 2359304 | tf_op jit(solution)/shard_map/ppermute | solution.py:79
  336.7 36.8 %collective-permute-start.27 = (bf16[192,2048]{1,0:T(8,128)(2,1)}, bf16[192,2048]{1,0:T(8,128)(2,1)}, u32[]{:S(2)}, u32[]{:S(2)}) collective-permute-start(bf16[192,2048]{1,0:T(8,128)(2,1)} %get-tuple-element.154), channel_id=1, source_target_pairs={{0,16},{4,20},{8,24},{12,28},{16,0},{20,4},{24,8},{28,12},{1,17},{... | collective-permute-start | bytes 2359304 | tf_op jit(solution)/shard_map/ppermute | solution.py:79
  338.1 35.3 %collective-permute-start.28 = (bf16[192,2048]{1,0:T(8,128)(2,1)}, bf16[192,2048]{1,0:T(8,128)(2,1)}, u32[]{:S(2)}, u32[]{:S(2)}) collective-permute-start(bf16[192,2048]{1,0:T(8,128)(2,1)} %get-tuple-element.155), channel_id=1, source_target_pairs={{0,24},{4,28},{8,16},{12,20},{16,8},{20,12},{24,0},{28,4},{1,25},{... | collective-permute-start | bytes 2359304 | tf_op jit(solution)/shard_map/ppermute | solution.py:79
  425.1 27.3 %collective-permute-start.32 = (bf16[192,2048]{1,0:T(8,128)(2,1)S(1)}, bf16[192,2048]{1,0:T(8,128)(2,1)S(1)}, u32[]{:S(2)}, u32[]{:S(2)}) collective-permute-start(bf16[192,2048]{1,0:T(8,128)(2,1)S(1)} %copy-done.70), channel_id=1, source_target_pairs={{0,24},{4,28},{8,16},{12,20},{16,8},{20,12},{24,0},{28,4},{1,25},{... | collective-permute-start | bytes 2359304 | tf_op jit(solution)/shard_map/ppermute | solution.py:79
  427.8 24.6 %collective-permute-start.35 = (bf16[384,256]{1,0:T(8,128)(2,1)S(1)}, bf16[384,256]{1,0:T(8,128)(2,1)S(1)}, u32[]{:S(2)}, u32[]{:S(2)}) collective-permute-start(bf16[384,256]{1,0:T(8,128)(2,1)S(1)} %get-tuple-element.216), channel_id=1, source_target_pairs={{1,0},{2,1},{3,2},{5,4},{6,5},{7,6},{9,8},{10,9},{11,10},{13,12},{... | collective-permute-start | bytes 589832 | tf_op jit(solution)/shard_map/ppermute | solution.py:85
  429.1 39.3 %collective-permute-start.36 = (bf16[384,256]{1,0:T(8,128)(2,1)S(1)}, bf16[384,256]{1,0:T(8,128)(2,1)S(1)}, u32[]{:S(2)}, u32[]{:S(2)}) collective-permute-start(bf16[384,256]{1,0:T(8,128)(2,1)S(1)} %get-tuple-element.215), channel_id=1, source_target_pairs={{2,0},{3,1},{6,4},{7,5},{10,8},{11,9},{14,12},{15,13},{18,16},{19,... | collective-permute-start | bytes 589832 | tf_op jit(solution)/shard_map/ppermute | solution.py:85
  474.0 29.0 %collective-permute-start.38 = (bf16[1024,640]{1,0:T(8,128)(2,1)S(1)}, bf16[1024,640]{1,0:T(8,128)(2,1)S(1)}, u32[]{:S(2)}, u32[]{:S(2)}) collective-permute-start(bf16[1024,640]{1,0:T(8,128)(2,1)S(1)} %qkv_grad_other.3), channel_id=1, source_target_pairs={{0,4},{4,0},{8,12},{12,8},{16,20},{20,16},{24,28},{28,24},{1,5},{5... | collective-permute-start | bytes 3932168 | tf_op jit(solution)/shard_map/ppermute | solution.py:79
  476.2 30.4 %collective-permute-start.37 = (bf16[1024,640]{1,0:T(8,128)(2,1)S(1)}, bf16[1024,640]{1,0:T(8,128)(2,1)S(1)}, u32[]{:S(2)}, u32[]{:S(2)}) collective-permute-start(bf16[1024,640]{1,0:T(8,128)(2,1)S(1)} %qkv_grad_other.2), channel_id=1, source_target_pairs={{0,4},{4,0},{8,12},{12,8},{16,20},{20,16},{24,28},{28,24},{1,5},{5... | collective-permute-start | bytes 3932168 | tf_op jit(solution)/shard_map/ppermute | solution.py:79
  478.2 24.9 %collective-permute-start.40 = (bf16[256,1024]{1,0:T(8,128)(2,1)S(1)}, bf16[256,1024]{1,0:T(8,128)(2,1)S(1)}, u32[]{:S(2)}, u32[]{:S(2)}) collective-permute-start(bf16[256,1024]{1,0:T(8,128)(2,1)S(1)} %get-tuple-element.183), channel_id=1, source_target_pairs={{0,16},{4,20},{8,24},{12,28},{16,0},{20,4},{24,8},{28,12},{1,17},{... | collective-permute-start | bytes 1572872 | tf_op jit(solution)/shard_map/ppermute | solution.py:79
  479.0 31.3 %collective-permute-start.42 = (bf16[256,1024]{1,0:T(8,128)(2,1)}, bf16[256,1024]{1,0:T(8,128)(2,1)}, u32[]{:S(2)}, u32[]{:S(2)}) collective-permute-start(bf16[256,1024]{1,0:T(8,128)(2,1)} %get-tuple-element.190), channel_id=1, source_target_pairs={{0,24},{4,28},{8,16},{12,20},{16,8},{20,12},{24,0},{28,4},{1,25},{... | collective-permute-start | bytes 1572872 | tf_op jit(solution)/shard_map/ppermute | solution.py:79
  521.0 29.2 %collective-permute-start.43 = (bf16[256,2816]{1,0:T(8,128)(2,1)S(1)}, bf16[256,2816]{1,0:T(8,128)(2,1)}, u32[]{:S(2)}, u32[]{:S(2)}) collective-permute-start(bf16[256,2816]{1,0:T(8,128)(2,1)S(1)} %copy-done.19), channel_id=1, source_target_pairs={{0,8},{4,12},{8,0},{12,4},{16,24},{20,28},{24,16},{28,20},{1,9},{5... | collective-permute-start | bytes 4325384 | tf_op jit(solution)/shard_map/ppermute | solution.py:79
  521.7 30.8 %collective-permute-start.44 = (bf16[256,2816]{1,0:T(8,128)(2,1)S(1)}, bf16[256,2816]{1,0:T(8,128)(2,1)}, u32[]{:S(2)}, u32[]{:S(2)}) collective-permute-start(bf16[256,2816]{1,0:T(8,128)(2,1)S(1)} %copy-done.19), channel_id=1, source_target_pairs={{0,16},{4,20},{8,24},{12,28},{16,0},{20,4},{24,8},{28,12},{1,17},{... | collective-permute-start | bytes 4325384 | tf_op jit(solution)/shard_map/ppermute | solution.py:79
  559.8 27.6 %collective-permute-start.48 = (bf16[256,2816]{1,0:T(8,128)(2,1)S(1)}, bf16[256,2816]{1,0:T(8,128)(2,1)S(1)}, u32[]{:S(2)}, u32[]{:S(2)}) collective-permute-start(bf16[256,2816]{1,0:T(8,128)(2,1)S(1)} %copy-done.19), channel_id=1, source_target_pairs={{0,4},{4,0},{8,12},{12,8},{16,20},{20,16},{24,28},{28,24},{1,5},{5... | collective-permute-start | bytes 4325384 | tf_op jit(solution)/shard_map/ppermute | solution.py:79
  559.8 41.1 %collective-permute-start.49 = (bf16[256,2816]{1,0:T(8,128)(2,1)}, bf16[256,2816]{1,0:T(8,128)(2,1)}, u32[]{:S(2)}, u32[]{:S(2)}) collective-permute-start(bf16[256,2816]{1,0:T(8,128)(2,1)} %collective-permute-done.43.refs_1_), channel_id=1, source_target_pairs={{0,4},{4,0},{8,12},{12,8},{16,20},{20,16},{24,28},{28,24},{1,5},{5... | collective-permute-start | bytes 4325384 | tf_op jit(solution)/shard_map/ppermute | solution.py:79
  560.3 24.2 %collective-permute-start.41 = (bf16[192,2048]{1,0:T(8,128)(2,1)S(1)}, bf16[192,2048]{1,0:T(8,128)(2,1)S(1)}, u32[]{:S(2)}, u32[]{:S(2)}) collective-permute-start(bf16[192,2048]{1,0:T(8,128)(2,1)S(1)} %get-tuple-element.187), channel_id=1, source_target_pairs={{0,8},{4,12},{8,0},{12,4},{16,24},{20,28},{24,16},{28,20},{1,9},{5... | collective-permute-start | bytes 2359304 | tf_op jit(solution)/shard_map/ppermute | solution.py:79
  562.8 38.2 %collective-permute-start.50 = (bf16[256,2816]{1,0:T(8,128)(2,1)}, bf16[256,2816]{1,0:T(8,128)(2,1)}, u32[]{:S(2)}, u32[]{:S(2)}) collective-permute-start(bf16[256,2816]{1,0:T(8,128)(2,1)} %collective-permute-done.44.refs_2_), channel_id=1, source_target_pairs={{0,4},{4,0},{8,12},{12,8},{16,20},{20,16},{24,28},{28,24},{1,5},{5... | collective-permute-start | bytes 4325384 | tf_op jit(solution)/shard_map/ppermute | solution.py:79
  567.7 33.4 %collective-permute-start.53 = (bf16[352,1024]{1,0:T(8,128)(2,1)}, bf16[352,1024]{1,0:T(8,128)(2,1)}, u32[]{:S(2)}, u32[]{:S(2)}) collective-permute-start(bf16[352,1024]{1,0:T(8,128)(2,1)} %reduce-scatter.4.cloned.1.call-done.refs_0_), channel_id=1, source_target_pairs={{0,8},{4,12},{8,0},{12,4},{16,24},{20,28},{24,16},{28,20},{1,9},{5... | collective-permute-start | bytes 2162696 | tf_op jit(solution)/shard_map/ppermute | solution.py:79
  584.5 31.5 %collective-permute-start.55 = (bf16[352,1024]{1,0:T(8,128)(2,1)}, bf16[352,1024]{1,0:T(8,128)(2,1)}, u32[]{:S(2)}, u32[]{:S(2)}) collective-permute-start(bf16[352,1024]{1,0:T(8,128)(2,1)} %reduce-scatter.4.cloned.1.call-done.refs_0_), channel_id=1, source_target_pairs={{0,16},{4,20},{8,24},{12,28},{16,0},{20,4},{24,8},{28,12},{1,17},{... | collective-permute-start | bytes 2162696 | tf_op jit(solution)/shard_map/ppermute | solution.py:79
  588.6 33.3 %collective-permute-start.57 = (bf16[352,1024]{1,0:T(8,128)(2,1)}, bf16[352,1024]{1,0:T(8,128)(2,1)}, u32[]{:S(2)}, u32[]{:S(2)}) collective-permute-start(bf16[352,1024]{1,0:T(8,128)(2,1)} %reduce-scatter.4.cloned.1.call-done.refs_0_), channel_id=1, source_target_pairs={{0,24},{4,28},{8,16},{12,20},{16,8},{20,12},{24,0},{28,4},{1,25},{... | collective-permute-start | bytes 2162696 | tf_op jit(solution)/shard_map/ppermute | solution.py:79
  600.9 19.9 %collective-permute-start.47 = (bf16[256,640]{1,0:T(8,128)(2,1)S(1)}, bf16[256,640]{1,0:T(8,128)(2,1)S(1)}, u32[]{:S(2)}, u32[]{:S(2)}) collective-permute-start(bf16[256,640]{1,0:T(8,128)(2,1)S(1)} %slice.38), channel_id=1, source_target_pairs={{0,16},{4,20},{8,24},{12,28},{16,0},{20,4},{24,8},{28,12},{1,17},{... | collective-permute-start | bytes 983048 | tf_op jit(solution)/shard_map/ppermute | solution.py:79
  601.0 21.5 %collective-permute-start.52 = (bf16[352,1024]{1,0:T(8,128)(2,1)}, bf16[352,1024]{1,0:T(8,128)(2,1)S(1)}, u32[]{:S(2)}, u32[]{:S(2)}) collective-permute-start(bf16[352,1024]{1,0:T(8,128)(2,1)} %reduce-scatter.4.cloned.1.call-done.refs_0_), channel_id=1, source_target_pairs={{0,4},{4,0},{8,12},{12,8},{16,20},{20,16},{24,28},{28,24},{1,5},{5... | collective-permute-start | bytes 2162696 | tf_op jit(solution)/shard_map/ppermute | solution.py:79
  601.1 22.1 %collective-permute-start.54 = (bf16[352,1024]{1,0:T(8,128)(2,1)}, bf16[352,1024]{1,0:T(8,128)(2,1)S(1)}, u32[]{:S(2)}, u32[]{:S(2)}) collective-permute-start(bf16[352,1024]{1,0:T(8,128)(2,1)} %collective-permute-done.53.refs_2_), channel_id=1, source_target_pairs={{0,4},{4,0},{8,12},{12,8},{16,20},{20,16},{24,28},{28,24},{1,5},{5... | collective-permute-start | bytes 2162696 | tf_op jit(solution)/shard_map/ppermute | solution.py:79
  620.8 42.7 %collective-permute-start.51 = (bf16[256,2816]{1,0:T(8,128)(2,1)}, bf16[256,2816]{1,0:T(8,128)(2,1)S(1)}, u32[]{:S(2)}, u32[]{:S(2)}) collective-permute-start(bf16[256,2816]{1,0:T(8,128)(2,1)} %copy-done.53), channel_id=1, source_target_pairs={{0,4},{4,0},{8,12},{12,8},{16,20},{20,16},{24,28},{28,24},{1,5},{5... | collective-permute-start | bytes 4325384 | tf_op jit(solution)/shard_map/ppermute | solution.py:79
  623.3 27.7 %collective-permute-start.62 = (bf16[256,1152]{1,0:T(8,128)(2,1)S(1)}, bf16[256,1152]{1,0:T(8,128)(2,1)}, u32[]{:S(2)}, u32[]{:S(2)}) collective-permute-start(bf16[256,1152]{1,0:T(8,128)(2,1)S(1)} %pad_maximum_fusion.1.refs_0_), channel_id=1, source_target_pairs={{0,16},{4,20},{8,24},{12,28},{16,0},{20,4},{24,8},{28,12},{1,17},{... | collective-permute-start | bytes 1769480 | tf_op jit(solution)/shard_map/ppermute | solution.py:79
  625.0 26.0 %collective-permute-start.64 = (bf16[256,1152]{1,0:T(8,128)(2,1)S(1)}, bf16[256,1152]{1,0:T(8,128)(2,1)}, u32[]{:S(2)}, u32[]{:S(2)}) collective-permute-start(bf16[256,1152]{1,0:T(8,128)(2,1)S(1)} %pad_maximum_fusion.1.refs_0_), channel_id=1, source_target_pairs={{0,24},{4,28},{8,16},{12,20},{16,8},{20,12},{24,0},{28,4},{1,25},{... | collective-permute-start | bytes 1769480 | tf_op jit(solution)/shard_map/ppermute | solution.py:79
  626.1 49.5 %collective-permute-start.59 = (bf16[256,1152]{1,0:T(8,128)(2,1)S(1)}, bf16[256,1152]{1,0:T(8,128)(2,1)S(1)}, u32[]{:S(2)}, u32[]{:S(2)}) collective-permute-start(bf16[256,1152]{1,0:T(8,128)(2,1)S(1)} %pad_maximum_fusion.1.refs_0_), channel_id=1, source_target_pairs={{0,4},{4,0},{8,12},{12,8},{16,20},{20,16},{24,28},{28,24},{1,5},{5... | collective-permute-start | bytes 1769480 | tf_op jit(solution)/shard_map/ppermute | solution.py:79
  638.9 36.7 %collective-permute-start.61 = (bf16[256,1152]{1,0:T(8,128)(2,1)}, bf16[256,1152]{1,0:T(8,128)(2,1)}, u32[]{:S(2)}, u32[]{:S(2)}) collective-permute-start(bf16[256,1152]{1,0:T(8,128)(2,1)} %collective-permute-done.60.refs_2_), channel_id=1, source_target_pairs={{0,4},{4,0},{8,12},{12,8},{16,20},{20,16},{24,28},{28,24},{1,5},{5... | collective-permute-start | bytes 1769480 | tf_op jit(solution)/shard_map/ppermute | solution.py:79
  651.0 24.6 %collective-permute-start.63 = (bf16[256,1152]{1,0:T(8,128)(2,1)}, bf16[256,1152]{1,0:T(8,128)(2,1)}, u32[]{:S(2)}, u32[]{:S(2)}) collective-permute-start(bf16[256,1152]{1,0:T(8,128)(2,1)} %collective-permute-done.62.refs_4_), channel_id=1, source_target_pairs={{0,4},{4,0},{8,12},{12,8},{16,20},{20,16},{24,28},{28,24},{1,5},{5... | collective-permute-start | bytes 1769480 | tf_op jit(solution)/shard_map/ppermute | solution.py:79
  651.0 24.6 %collective-permute-start.65 = (bf16[256,1152]{1,0:T(8,128)(2,1)}, bf16[256,1152]{1,0:T(8,128)(2,1)}, u32[]{:S(2)}, u32[]{:S(2)}) collective-permute-start(bf16[256,1152]{1,0:T(8,128)(2,1)} %collective-permute-done.64.refs_6_), channel_id=1, source_target_pairs={{0,4},{4,0},{8,12},{12,8},{16,20},{20,16},{24,28},{28,24},{1,5},{5... | collective-permute-start | bytes 1769480 | tf_op jit(solution)/shard_map/ppermute | solution.py:79
  (97 other events, 1123.3 us)
Sparse Core Ops, SparseCore 0:
  13.1 35.3 all-gather.4
  50.6 27.8 all-gather.6
  80.7 113.7 all-gather.8
  202.7 63.0 all-gather.10
  297.1 54.8 reduce-scatter.3
  354.7 114.2 reduce-scatter.5
  519.8 65.6 reduce-scatter.7
where the time goes:
time: 705 us; the launch traced here: 696 us
  waiting for transfers between devices  306 us (43%)
  Pallas kernels  252 us (36%)
  starting transfers between devices  74.8 us (11%)
  local copies, waits for them, and re-layouts  42.8 us (6%)
  between operations  15.2 us (2%)
    ppermute x57, waiting for transfers between devices, swap(): return lax.ppermute(value, 'replica', [(i, i ^ mask) for i in range(size)])  235 us
    pallas_call x21, Pallas kernels, kernel_call(): return pl.pallas_call(body, grid_spec=spec, **common)(*operands)  147 us
    pallas_call x19, Pallas kernels, kernel_call(): return pl.pallas_call(body, grid_spec=spec, **common)(index, *operands)  105 us
    ppermute x57, starting transfers between devices, swap(): return lax.ppermute(value, 'replica', [(i, i ^ mask) for i in range(size)])  45.4 us
    ppermute x9, waiting for transfers between devices, shift(): return lax.ppermute(value, 'shard', pairs)  33 us
    all_gather x1, waiting for transfers between devices, per_device(): lax.all_gather(down_block(index, down_weight, local), 'shard', axis=0, ti...  32.3 us
    unnamed x148, local copies, waits for them, and re-layouts  29.6 us
    ppermute x9, starting transfers between devices, shift(): return lax.ppermute(value, 'shard', pairs)  28.9 us
  transfers between devices with their start and end apart: 73, of which 32 were waited for; matrix products, arithmetic and copies ran while one was open for 2% of the time, Pallas kernels for 30%

commit v1 on v0

--- a/solution.py
+++ b/solution.py
@@ -47,7 +47,7 @@
     return pl.BlockSpec(memory_space=VMEM)
 
 
-TIMES = {"attention_back": 13.0}
+TIMES = {"attention_back": 13.0, "feedforward_result": 10.0, "down_result": 8.0, "grad_input": 4.0}
 
 
 def kernel_call(body, out_shape, in_specs, out_specs, operands, *, index=None, grid=(), scratch=(),
@@ -1255,7 +1255,6 @@
     gu_mine = gu_mine[:3] + [jnp.concatenate(gu_mine[3:], axis=0)]
     gu_theirs = [swap(after(part, output), 1) for part in gu_mine]
     gu_out = feedforward_result(index, 0, gu_mine, gate_weight, up_weight, gain_two, ff_local, None)
-    at_kept = after(at_kept, gu_out[0])
     gu_out = feedforward_result(index, 1, gu_theirs, gate_weight, up_weight, gain_two, ff_local, gu_out)
 
     down_mine = plane_gather(after(down_kept, *gu_mine[1:]))
@@ -1266,8 +1265,9 @@
     second = swap(at_kept[:, qkv_width : 2 * qkv_width], 4)
     first = at_kept[:, :qkv_width].astype(f32) + second.astype(f32)
     at_kept = jnp.concatenate([first.astype(bf16), at_kept[:, 2 * qkv_width :]], axis=1)
-    at_pieces = mixed(*plane_pieces(at_kept))
-    at_pieces[0] = after(at_pieces[0], gu_out[0], down_out, grad_input)
+    at_mine = plane_gather(at_kept)
+    at_near = [after(piece, gu_out[0], down_out, grad_input) for piece in at_mine]
+    at_pieces = mixed(at_mine, [swap(piece, 1) for piece in at_near])
     wo_out = out_result(index, at_pieces, local, width, qkv_width)
     q_out, k_out, v_out, gain_one_sums = qkv_result(
         index, at_pieces, query_weight, key_weight, value_weight, gain_one

time: 705 us -> 700 us (level)
    ppermute x57, waiting for transfers between devices: 235 us -> 226 us  [swap(): return lax.ppermute(value, 'replica', [(i, i ^ mask) for i in range(size)])]
    unnamed x148 -> x152, local copies, waits for them, and re-layouts: 29.6 us -> 28.8 us
  transfers between devices with their start and end apart: 73 -> 73, of which waited for: 32 -> 36; matrix products, arithmetic and copies ran while one was open for 2% -> 3% of each run, Pallas kernels for 30% -> 31%
where the time goes in v1:
time: 700 us; the launch traced here: 691 us
  waiting for transfers between devices  300 us (43%)
  Pallas kernels  252 us (36%)
  starting transfers between devices  75.7 us (11%)
  local copies, waits for them, and re-layouts  42.9 us (6%)
  between operations  15.2 us (2%)
    ppermute x57, waiting for transfers between devices, swap(): return lax.ppermute(value, 'replica', [(i, i ^ mask) for i in range(size)])  226 us
    pallas_call x21, Pallas kernels, kernel_call(): return pl.pallas_call(body, grid_spec=spec, **common)(*operands)  147 us
    pallas_call x19, Pallas kernels, kernel_call(): return pl.pallas_call(body, grid_spec=spec, **common)(index, *operands)  105 us
    ppermute x57, starting transfers between devices, swap(): return lax.ppermute(value, 'replica', [(i, i ^ mask) for i in range(size)])  46.2 us
    ppermute x9, waiting for transfers between devices, shift(): return lax.ppermute(value, 'shard', pairs)  33.1 us
    all_gather x1, waiting for transfers between devices, per_device(): lax.all_gather(down_block(index, down_weight, local), 'shard', axis=0, ti...  32.4 us
    ppermute x9, starting transfers between devices, shift(): return lax.ppermute(value, 'shard', pairs)  29 us
    unnamed x152, local copies, waits for them, and re-layouts  28.8 us
  transfers between devices with their start and end apart: 73, of which 36 were waited for; matrix products, arithmetic and copies ran while one was open for 3% of the time, Pallas kernels for 31%

profile of v1, /device:TPU:0, one launch (start us, length us, event | category | flops | bytes accessed | tf_op | source)
XLA Modules:
  0.0 691.1 jit_solution(11972065924509716924)
XLA Ops:
  13.9 5.2 feedforward_block.1
  25.5 15.7 %collective-permute-done.refs_1_ = bf16[192,2048]{1,0:T(8,128)(2,1)S(1)} collective-permute-done((bf16[192,2048]{1,0:T(8,128)(2,1)S(1)}, bf16[192,2048]{1,0:T(8,128)(2,1)S(1)}, u32[]{:S(2)}, u32[]{:S(2)}) %collective-permute-start) | collective-permute-done | bytes 786464 | tf_op jit(solution)/shard_map/ppermute | solution.py:79
  41.2 16.0 %collective-permute-done.1 = bf16[192,2048]{1,0:T(8,128)(2,1)S(1)} collective-permute-done((bf16[192,2048]{1,0:T(8,128)(2,1)S(1)}, bf16[192,2048]{1,0:T(8,128)(2,1)S(1)}, u32[]{:S(2)}, u32[]{:S(2)}) %collective-permute-start.1) | collective-permute-done | bytes 786464 | tf_op jit(solution)/shard_map/ppermute | solution.py:79
  61.5 4.1 qkv.2
  70.1 4.5 collective-permute-start.5
  75.9 13.6 %collective-permute-done.7.refs_1_.refs_3_ = bf16[1024,640]{1,0:T(8,128)(2,1)S(1)} collective-permute-done((bf16[1024,640]{1,0:T(8,128)(2,1)}, bf16[1024,640]{1,0:T(8,128)(2,1)S(1)}, u32[]{:S(2)}, u32[]{:S(2)}) %collective-permute-start.7) | collective-permute-done | bytes 1310752 | tf_op jit(solution)/shard_map/ppermute | solution.py:79
  103.7 4.5 collective-permute-start.10
  108.8 7.3 %collective-permute-start.11 = (bf16[384,128]{1,0:T(8,128)(2,1)S(1)}, bf16[384,128]{1,0:T(8,128)(2,1)S(1)}, u32[]{:S(2)}, u32[]{:S(2)}) collective-permute-start(bf16[384,128]{1,0:T(8,128)(2,1)S(1)} %get-tuple-element.124.refs_0_.refs_10_), channel_id=1, source_target_pairs={{0,3},{4,7},{8,11},{12,15},{16,19},{20,23},{24,27},{28,31}} | collective-permute-start | bytes 294920 | tf_op jit(solution)/shard_map/ppermute | solution.py:85
  116.2 4.6 collective-permute-done.11.refs_3_.refs_13_
  127.1 4.5 attention.2
  131.6 4.5 attention.3
  138.3 7.4 %attention_out.1 = (f32[192,2048]{1,0:T(8,128)}, bf16[192,2048]{1,0:T(8,128)(2,1)S(1)}) custom-call(bf16[384,512]{1,0:T(8,128)(2,1)S(1)} %get-tuple-element.120.refs_0_, bf16[384,512]{1,0:T(8,128)(2,1)S(1)} %get-tuple-element.125.refs_1_, bf16[1024,1024]{1,0:T(8,128)(2,1)} %out_rows.1.refs_2_.refs_3_.wo_own, ...), custom_call_target="tpu_custom_call" | custom-call | tf_op jit(solution)/shard_map/attention_out/pallas_call | solution.py:69
  148.2 17.2 %collective-permute-done.16.refs_1_ = bf16[192,2048]{1,0:T(8,128)(2,1)S(1)} collective-permute-done((bf16[192,2048]{1,0:T(8,128)(2,1)S(1)}, bf16[192,2048]{1,0:T(8,128)(2,1)S(1)}, u32[]{:S(2)}, u32[]{:S(2)}) %collective-permute-start.16) | collective-permute-done | bytes 786464 | tf_op jit(solution)/shard_map/ppermute | solution.py:79
  169.7 17.7 %collective-permute-done.18.refs_1_ = bf16[192,2048]{1,0:T(8,128)(2,1)S(1)} collective-permute-done((bf16[192,2048]{1,0:T(8,128)(2,1)S(1)}, bf16[192,2048]{1,0:T(8,128)(2,1)S(1)}, u32[]{:S(2)}, u32[]{:S(2)}) %collective-permute-start.18) | collective-permute-done | bytes 786464 | tf_op jit(solution)/shard_map/ppermute | solution.py:79
  202.8 6.6 collective-permute-done.22.refs_7_.refs_8_.refs_2_
  209.4 17.0 %gate.3 = (bf16[768,1408]{1,0:T(8,128)(2,1)}, bf16[768,1408]{1,0:T(8,128)(2,1)}, bf16[768,1408]{1,0:T(8,128)(2,1)}, bf16[768,2048]{1,0:T(8,128)(2,1)}) custom-call(bf16[192,2048]{1,0:T(8,128)(2,1)S(1)} %get-tuple-element.140.refs_0_, bf16[192,2048]{1,0:T(8,128)(2,1)} %copy-done.57, bf16[192,2048]{1,0:T(8,128)(2,1)} %copy-done.58, ...), custom_call_target="tpu_custom_call" | custom-call | tf_op jit(solution)/shard_map/gate/pallas_call | solution.py:69
  226.5 6.8 down_grad_other.1
  233.5 32.4 %all-gather.11.cloned.1.call-done.own.refs_1_ = bf16[1408,1024]{1,0:T(8,128)(2,1)} async-done(((bf16[352,1024]{1,0:T(8,128)(2,1)}), bf16[1408,1024]{1,0:T(8,128)(2,1)}) %all-gather.11.cloned.1.call-update) | async-done | bytes 2883600 | tf_op jit(solution)/shard_map/all_gather | solution.py:1125
  265.8 7.3 %down_grad.1 = bf16[1408,1024]{1,0:T(8,128)(2,1)} custom-call(bf16[768,1408]{1,0:T(8,128)(2,1)} %get-tuple-element.150.left.refs_0_, bf16[768,2048]{1,0:T(8,128)(2,1)} %copy-done.52, bf16[1408,1024]{1,0:T(8,128)(2,1)} %collective-permute-done.23.refs_0_), custom_call_target="tpu_custom_call" | custom-call | tf_op jit(solution)/shard_map/down_grad/pallas_call | solution.py:69
  273.1 11.0 %hidden_back.1.right.refs_0_ = bf16[768,2816]{1,0:T(8,128)(2,1)} custom-call(bf16[768,2048]{1,0:T(8,128)(2,1)} %copy-done.52, bf16[1408,1024]{1,0:T(8,128)(2,1)} %all-gather.11.cloned.1.call-done.own.refs_1_, bf16[1408,1024]{1,0:T(8,128)(2,1)} %collective-permute-done.24.other.refs_2_, bf16[768,1408]{1,0:T(8,128)(2,1)} %get-tuple-element.145.for_gate, ...), custom_call_target="tpu_custom_call" | custom-call | tf_op jit(solution)/shard_map/hidden_back/pallas_call | solution.py:69
  284.1 12.3 %gate_grad_other.1 = bf16[1024,2816]{1,0:T(8,128)(2,1)} custom-call(bf16[768,2048]{1,0:T(8,128)(2,1)} %get-tuple-element.147.left, bf16[768,2816]{1,0:T(8,128)(2,1)} %hidden_back.1.right.refs_0_), custom_call_target="tpu_custom_call" | custom-call | tf_op jit(solution)/shard_map/gate_grad_other/pallas_call | solution.py:69
  297.0 9.3 %collective-permute-done.25.refs_0_ = bf16[1024,2816]{1,0:T(8,128)(2,1)} collective-permute-done((bf16[1024,2816]{1,0:T(8,128)(2,1)}, bf16[1024,2816]{1,0:T(8,128)(2,1)}, u32[]{:S(2)}, u32[]{:S(2)}) %collective-permute-start.25) | collective-permute-done | bytes 5767200 | tf_op jit(solution)/shard_map/ppermute | solution.py:79
  306.3 13.4 %gate_grad.1 = bf16[1024,2816]{1,0:T(8,128)(2,1)} custom-call(bf16[768,2048]{1,0:T(8,128)(2,1)} %get-tuple-element.147.left, bf16[768,2816]{1,0:T(8,128)(2,1)} %hidden_back.1.right.refs_0_, bf16[1024,2816]{1,0:T(8,128)(2,1)} %collective-permute-done.25.refs_0_), custom_call_target="tpu_custom_call" | custom-call | tf_op jit(solution)/shard_map/gate_grad/pallas_call | solution.py:69
  319.8 15.4 %feedforward_back.1 = (f32[192,2048]{1,0:T(8,128)}, bf16[192,2048]{1,0:T(8,128)(2,1)}, bf16[192,2048]{1,0:T(8,128)(2,1)}, bf16[192,2048]{1,0:T(8,128)(2,1)}) custom-call(bf16[768,2816]{1,0:T(8,128)(2,1)} %hidden_back.1.right.refs_0_, bf16[1024,2816]{1,0:T(8,128)(2,1)} %all-gather.9.cloned.1.call-done.refs_5_.refs_6_.refs_1_, ...), custom_call_target="tpu_custom_call" | custom-call | tf_op jit(solution)/shard_map/feedforward_back/pallas_call | solution.py:69
  338.7 11.0 %feedforward_out.1 = (f32[192,2048]{1,0:T(8,128)}, bf16[192,2048]{1,0:T(8,128)(2,1)S(1)}, bf16[192,2048]{1,0:T(8,128)(2,1)S(1)}, bf16[192,2048]{1,0:T(8,128)(2,1)}) custom-call(bf16[768,1408]{1,0:T(8,128)(2,1)} %get-tuple-element.150.left.refs_0_, bf16[1408,1024]{1,0:T(8,128)(2,1)} %all-gather.11.cloned.1.call-done.own.refs_1_, ...), custom_call_target="tpu_custom_call" | custom-call | tf_op jit(solution)/shard_map/feedforward_out/pallas_call | solution.py:69
  356.7 16.8 %collective-permute-done.27.refs_2_ = bf16[192,2048]{1,0:T(8,128)(2,1)} collective-permute-done((bf16[192,2048]{1,0:T(8,128)(2,1)}, bf16[192,2048]{1,0:T(8,128)(2,1)}, u32[]{:S(2)}, u32[]{:S(2)}) %collective-permute-start.27) | collective-permute-done | bytes 786464 | tf_op jit(solution)/shard_map/ppermute | solution.py:79
  374.6 4.8 grad_middle.1
  385.3 13.2 %attention_back.2 = (bf16[384,1024]{1,0:T(8,128)(2,1)}, f32[384,256]{1,0:T(8,128)S(1)}, bf16[3,384,256]{2,1,0:T(8,128)(2,1)}) custom-call(s32[3]{0:T(128)S(1)} %pad_add_fusion.index, bf16[192,2048]{1,0:T(8,128)(2,1)} %copy-done.9, bf16[1024,1024]{1,0:T(8,128)(2,1)} %out_rows.1.refs_2_.refs_3_.wo_own, bf16[1024,1024]{1,0:T(8,128)(2,1)} %copy-done.51, ...), custom_call_target="tpu_custom_call" | custom-call | bytes 47970000 | tf_op jit(solution)/shard_map/attention_back/pallas_call | solution.py:74
  400.9 13.3 %attention_back.3 = (bf16[384,1024]{1,0:T(8,128)(2,1)}, f32[384,256]{1,0:T(8,128)S(1)}, bf16[3,384,256]{2,1,0:T(8,128)(2,1)}) custom-call(s32[3]{0:T(128)S(1)} %pad_add_fusion.index, bf16[192,2048]{1,0:T(8,128)(2,1)} %collective-permute-done.29.branch, ...), custom_call_target="tpu_custom_call", output_to_operand_aliasing={{0}: (20, {}), {1}: (21, {}), {2}: (22, {})} | custom-call | bytes 47970000 | tf_op jit(solution)/shard_map/attention_back/pallas_call | solution.py:74
  420.4 4.7 out_grad_other.1
  430.4 11.8 %collective-permute-done.34.refs_2_ = bf16[384,256]{1,0:T(8,128)(2,1)S(1)} collective-permute-done((bf16[384,256]{1,0:T(8,128)(2,1)S(1)}, bf16[384,256]{1,0:T(8,128)(2,1)S(1)}, u32[]{:S(2)}, u32[]{:S(2)}) %collective-permute-start.34) | collective-permute-done | bytes 196640 | tf_op jit(solution)/shard_map/ppermute | solution.py:85
  443.5 5.0 out_grad.1.term
  452.4 16.1 %collective-permute-done.36.refs_1_ = bf16[384,256]{1,0:T(8,128)(2,1)S(1)} collective-permute-done((bf16[384,256]{1,0:T(8,128)(2,1)S(1)}, bf16[384,256]{1,0:T(8,128)(2,1)S(1)}, u32[]{:S(2)}, u32[]{:S(2)}) %collective-permute-start.36) | collective-permute-done | bytes 196640 | tf_op jit(solution)/shard_map/ppermute | solution.py:85
  480.3 11.3 %collective-permute-done.39.refs_1_ = bf16[256,1024]{1,0:T(8,128)(2,1)S(1)} collective-permute-done((bf16[256,1024]{1,0:T(8,128)(2,1)S(1)}, bf16[256,1024]{1,0:T(8,128)(2,1)S(1)}, u32[]{:S(2)}, u32[]{:S(2)}) %collective-permute-start.39) | collective-permute-done | bytes 524320 | tf_op jit(solution)/shard_map/ppermute | solution.py:79
  491.6 11.5 %collective-permute-done.40.refs_2_ = bf16[256,1024]{1,0:T(8,128)(2,1)S(1)} collective-permute-done((bf16[256,1024]{1,0:T(8,128)(2,1)S(1)}, bf16[256,1024]{1,0:T(8,128)(2,1)S(1)}, u32[]{:S(2)}, u32[]{:S(2)}) %collective-permute-start.40) | collective-permute-done | bytes 524320 | tf_op jit(solution)/shard_map/ppermute | solution.py:79
  521.9 8.1 %qkv_back.1 = (f32[192,2048]{1,0:T(8,128)}, bf16[192,2048]{1,0:T(8,128)(2,1)S(1)}) custom-call(bf16[384,640]{1,0:T(8,128)(2,1)S(1)} %get-tuple-element.187.right.refs_0_, bf16[384,640]{1,0:T(8,128)(2,1)S(1)} %copy-done.5, bf16[1024,640]{1,0:T(8,128)(2,1)} %all-gather.5.cloned.1.call-done.refs_2_, bf16[1024,640]{1,0:T(8,128)(2,1)} %copy-done.3, ...), custom_call_target="tpu_custom_call" | custom-call | tf_op jit(solution)/shard_map/qkv_back/pallas_call | solution.py:69
  530.0 19.2 %collective-permute-done.45.refs_1_ = bf16[256,2816]{1,0:T(8,128)(2,1)} collective-permute-done((bf16[256,2816]{1,0:T(8,128)(2,1)}, bf16[256,2816]{1,0:T(8,128)(2,1)}, u32[]{:S(2)}, u32[]{:S(2)}) %collective-permute-start.45) | collective-permute-done | bytes 1441824 | tf_op jit(solution)/shard_map/ppermute | solution.py:79
  554.4 4.4 output.1
  569.4 13.5 %collective-permute-done.41.refs_1_ = bf16[192,2048]{1,0:T(8,128)(2,1)S(1)} collective-permute-done((bf16[192,2048]{1,0:T(8,128)(2,1)S(1)}, bf16[192,2048]{1,0:T(8,128)(2,1)S(1)}, u32[]{:S(2)}, u32[]{:S(2)}) %collective-permute-start.41) | collective-permute-done | bytes 786464 | tf_op jit(solution)/shard_map/ppermute | solution.py:79
  591.1 7.3 %collective-permute-done.53.refs_2_ = bf16[352,1024]{1,0:T(8,128)(2,1)} collective-permute-done((bf16[352,1024]{1,0:T(8,128)(2,1)}, bf16[352,1024]{1,0:T(8,128)(2,1)}, u32[]{:S(2)}, u32[]{:S(2)}) %collective-permute-start.53) | collective-permute-done | bytes 720928 | tf_op jit(solution)/shard_map/ppermute | solution.py:79
  598.5 13.3 %collective-permute-done.43 = bf16[256,640]{1,0:T(8,128)(2,1)S(1)} collective-permute-done((bf16[256,640]{1,0:T(8,128)(2,1)S(1)}, bf16[256,640]{1,0:T(8,128)(2,1)S(1)}, u32[]{:S(2)}, u32[]{:S(2)}) %collective-permute-start.43) | collective-permute-done | bytes 327712 | tf_op jit(solution)/shard_map/ppermute | solution.py:79
  612.8 14.1 %collective-permute-done.55.refs_4_ = bf16[352,1024]{1,0:T(8,128)(2,1)S(1)} collective-permute-done((bf16[352,1024]{1,0:T(8,128)(2,1)}, bf16[352,1024]{1,0:T(8,128)(2,1)S(1)}, u32[]{:S(2)}, u32[]{:S(2)}) %collective-permute-start.55) | collective-permute-done | bytes 720928 | tf_op jit(solution)/shard_map/ppermute | solution.py:79
  631.1 4.1 grad_input.1
  635.2 10.6 %feedforward_result.2 = (f32[512,5632]{1,0:T(8,128)}, f32[512,5632]{1,0:T(8,128)}, f32[512,128]{1,0:T(8,128)S(1)}) custom-call(s32[3]{0:T(128)S(1)} %pad_add_fusion.index, bf16[256,2816]{1,0:T(8,128)(2,1)} %reduce-scatter.6.cloned.1.call-done.refs_0_, bf16[256,2816]{1,0:T(8,128)(2,1)} %collective-permute-done.45.refs_1_, ...), custom_call_target="tpu_custom_call" | custom-call | bytes 36900000 | tf_op jit(solution)/shard_map/feedforward_result/pallas_call | solution.py:74
  645.8 10.2 %feedforward_result.3 = (f32[512,5632]{1,0:T(8,128)}, f32[512,5632]{1,0:T(8,128)}, f32[512,128]{1,0:T(8,128)S(1)}) custom-call(s32[3]{0:T(128)S(1)} %pad_add_fusion.index, bf16[256,2816]{1,0:T(8,128)(2,1)S(1)} %copy-done.20, bf16[256,2816]{1,0:T(8,128)(2,1)} %collective-permute-done.46.refs_1_, ...), custom_call_target="tpu_custom_call", output_to_operand_aliasing={{0}: (8, {}), {1}: (9, {}), {2}: (10, {})} | custom-call | bytes 36900000 | tf_op jit(solution)/shard_map/feedforward_result/pallas_call | solution.py:74
  657.8 7.6 %down_result.1 = f32[1408,2048]{1,0:T(8,128)} custom-call(s32[3]{0:T(128)S(1)} %pad_add_fusion.index, bf16[352,1024]{1,0:T(8,128)(2,1)} %reduce-scatter.4.cloned.1.call-done.refs_0_, bf16[352,1024]{1,0:T(8,128)(2,1)S(1)} %collective-permute-done.52.refs_1_, bf16[352,1024]{1,0:T(8,128)(2,1)} %collective-permute-done.53.refs_2_, bf16[352,1024]{1,0:T(8,128)(2,1)} %copy-done.67, ...), custom_call_target="tpu_custom_call" | custom-call | bytes 29520000 | tf_op jit(solution)/shard_map/down_result/pallas_call | solution.py:74
  670.3 6.0 qkv_result.1
  679.2 4.9 out_result.1
  (326 shorter events, 174.8 us)
Async XLA Ops:
  7.2 50.1 %all-gather.5.cloned.1.call-start = ((), (), s32[]{:S(2)}) async-start(), calls=%async_computation.3 | async-start | bytes 1638400 | tf_op jit(solution)/shard_map/all_gather | solution.py:1121
  13.0 77.9 %all-gather.7.cloned.1.call-start = ((), (), s32[]{:S(2)}) async-start(), calls=%async_computation.4 | async-start | bytes 1310720 | tf_op jit(solution)/shard_map/all_gather | solution.py:1122
  13.7 180.7 %all-gather.9.cloned.1.call-start = ((), (), s32[]{:S(2)}) async-start(), calls=%async_computation.5 | async-start | bytes 7208960 | tf_op jit(solution)/shard_map/all_gather | solution.py:1124
  19.1 246.7 %all-gather.11.cloned.1.call-start = ((), (), s32[]{:S(2)}) async-start(), calls=%async_computation.6 | async-start | bytes 3604480 | tf_op jit(solution)/shard_map/all_gather | solution.py:1125
  19.8 21.4 %collective-permute-start = (bf16[192,2048]{1,0:T(8,128)(2,1)S(1)}, bf16[192,2048]{1,0:T(8,128)(2,1)S(1)}, u32[]{:S(2)}, u32[]{:S(2)}) collective-permute-start(bf16[192,2048]{1,0:T(8,128)(2,1)S(1)} %own_first.2.refs_0_.refs_2_), channel_id=1, source_target_pairs={{0,8},{4,12},{8,0},{12,4},{16,24},{20,28},{24,16},{28,20},{1,9},{5... | collective-permute-start | bytes 2359304 | tf_op jit(solution)/shard_map/ppermute | solution.py:79
  23.4 33.8 %collective-permute-start.1 = (bf16[192,2048]{1,0:T(8,128)(2,1)S(1)}, bf16[192,2048]{1,0:T(8,128)(2,1)S(1)}, u32[]{:S(2)}, u32[]{:S(2)}) collective-permute-start(bf16[192,2048]{1,0:T(8,128)(2,1)S(1)} %own_first.3.refs_5_), channel_id=1, source_target_pairs={{0,8},{4,12},{8,0},{12,4},{16,24},{20,28},{24,16},{28,20},{1,9},{5... | collective-permute-start | bytes 2359304 | tf_op jit(solution)/shard_map/ppermute | solution.py:79
  23.9 33.4 %collective-permute-start.2 = (bf16[192,2048]{1,0:T(8,128)(2,1)S(1)}, bf16[192,2048]{1,0:T(8,128)(2,1)}, u32[]{:S(2)}, u32[]{:S(2)}) collective-permute-start(bf16[192,2048]{1,0:T(8,128)(2,1)S(1)} %own_first.3.refs_5_), channel_id=1, source_target_pairs={{0,16},{4,20},{8,24},{12,28},{16,0},{20,4},{24,8},{28,12},{1,17},{... | collective-permute-start | bytes 2359304 | tf_op jit(solution)/shard_map/ppermute | solution.py:79
  58.1 31.4 %collective-permute-start.7 = (bf16[1024,640]{1,0:T(8,128)(2,1)}, bf16[1024,640]{1,0:T(8,128)(2,1)S(1)}, u32[]{:S(2)}, u32[]{:S(2)}) collective-permute-start(bf16[1024,640]{1,0:T(8,128)(2,1)} %all-gather.5.cloned.1.call-done.refs_2_), channel_id=1, source_target_pairs={{0,16},{4,20},{8,24},{12,28},{16,0},{20,4},{24,8},{28,12},{1,17},{... | collective-permute-start | bytes 3932168 | tf_op jit(solution)/shard_map/ppermute | solution.py:79
  66.3 23.2 %collective-permute-start.4 = (bf16[384,128]{1,0:T(8,128)(2,1)S(1)}, bf16[384,128]{1,0:T(8,128)(2,1)S(1)}, u32[]{:S(2)}, u32[]{:S(2)}) collective-permute-start(bf16[384,128]{1,0:T(8,128)(2,1)S(1)} %get-tuple-element.119.refs_0_.refs_3_), channel_id=1, source_target_pairs={{0,1},{1,2},{2,3},{4,5},{5,6},{6,7},{8,9},{9,10},{10,11},{12,13},{... | collective-permute-start | bytes 294920 | tf_op jit(solution)/shard_map/ppermute | solution.py:85
  70.1 19.5 %collective-permute-start.5 = (bf16[384,128]{1,0:T(8,128)(2,1)S(1)}, bf16[384,128]{1,0:T(8,128)(2,1)S(1)}, u32[]{:S(2)}, u32[]{:S(2)}) collective-permute-start(bf16[384,128]{1,0:T(8,128)(2,1)S(1)} %get-tuple-element.119.refs_0_.refs_3_), channel_id=1, source_target_pairs={{0,2},{1,3},{4,6},{5,7},{8,10},{9,11},{12,14},{13,15},{16,18},{17,... | collective-permute-start | bytes 294920 | tf_op jit(solution)/shard_map/ppermute | solution.py:85
  92.7 28.0 %collective-permute-start.12 = (bf16[256,1024]{1,0:T(8,128)(2,1)S(1)}, bf16[256,1024]{1,0:T(8,128)(2,1)S(1)}, u32[]{:S(2)}, u32[]{:S(2)}) collective-permute-start(bf16[256,1024]{1,0:T(8,128)(2,1)S(1)} %get-tuple-element.217), channel_id=1, source_target_pairs={{0,8},{4,12},{8,0},{12,4},{16,24},{20,28},{24,16},{28,20},{1,9},{5... | collective-permute-start | bytes 1572872 | tf_op jit(solution)/shard_map/ppermute | solution.py:79
  94.5 26.3 %collective-permute-start.13 = (bf16[256,1024]{1,0:T(8,128)(2,1)S(1)}, bf16[256,1024]{1,0:T(8,128)(2,1)S(1)}, u32[]{:S(2)}, u32[]{:S(2)}) collective-permute-start(bf16[256,1024]{1,0:T(8,128)(2,1)S(1)} %get-tuple-element.216), channel_id=1, source_target_pairs={{0,16},{4,20},{8,24},{12,28},{16,0},{20,4},{24,8},{28,12},{1,17},{... | collective-permute-start | bytes 1572872 | tf_op jit(solution)/shard_map/ppermute | solution.py:79
  95.9 24.9 %collective-permute-start.14 = (bf16[256,1024]{1,0:T(8,128)(2,1)S(1)}, bf16[256,1024]{1,0:T(8,128)(2,1)S(1)}, u32[]{:S(2)}, u32[]{:S(2)}) collective-permute-start(bf16[256,1024]{1,0:T(8,128)(2,1)S(1)} %get-tuple-element.215), channel_id=1, source_target_pairs={{0,24},{4,28},{8,16},{12,20},{16,8},{20,12},{24,0},{28,4},{1,25},{... | collective-permute-start | bytes 1572872 | tf_op jit(solution)/shard_map/ppermute | solution.py:79
  124.8 21.5 %collective-permute-start.17 = (bf16[192,2048]{1,0:T(8,128)(2,1)S(1)}, bf16[192,2048]{1,0:T(8,128)(2,1)S(1)}, u32[]{:S(2)}, u32[]{:S(2)}) collective-permute-start(bf16[192,2048]{1,0:T(8,128)(2,1)S(1)} %own_first.3.refs_5_), channel_id=1, source_target_pairs={{0,24},{4,28},{8,16},{12,20},{16,8},{20,12},{24,0},{28,4},{1,25},{... | collective-permute-start | bytes 2359304 | tf_op jit(solution)/shard_map/ppermute | solution.py:79
  145.7 19.7 %collective-permute-start.16 = (bf16[192,2048]{1,0:T(8,128)(2,1)S(1)}, bf16[192,2048]{1,0:T(8,128)(2,1)S(1)}, u32[]{:S(2)}, u32[]{:S(2)}) collective-permute-start(bf16[192,2048]{1,0:T(8,128)(2,1)S(1)} %get-tuple-element.133), channel_id=1, source_target_pairs={{0,8},{4,12},{8,0},{12,4},{16,24},{20,28},{24,16},{28,20},{1,9},{5... | collective-permute-start | bytes 2359304 | tf_op jit(solution)/shard_map/ppermute | solution.py:79
  169.1 19.8 %collective-permute-start.19 = (bf16[192,2048]{1,0:T(8,128)(2,1)S(1)}, bf16[192,2048]{1,0:T(8,128)(2,1)S(1)}, u32[]{:S(2)}, u32[]{:S(2)}) collective-permute-start(bf16[192,2048]{1,0:T(8,128)(2,1)S(1)} %get-tuple-element.140.refs_0_), channel_id=1, source_target_pairs={{0,16},{4,20},{8,24},{12,28},{16,0},{20,4},{24,8},{28,12},{1,17},{... | collective-permute-start | bytes 2359304 | tf_op jit(solution)/shard_map/ppermute | solution.py:79
  202.5 149.4 %reduce-scatter.4.cloned.1.call-start = ((), (), s32[]{:S(2)}) async-start(), calls=%async_computation.7 | async-start | bytes 3604480 | tf_op jit(solution)/shard_map/reduce_scatter | solution.py:1185
  233.3 32.5 %collective-permute-start.23 = (bf16[1408,1024]{1,0:T(8,128)(2,1)}, bf16[1408,1024]{1,0:T(8,128)(2,1)}, u32[]{:S(2)}, u32[]{:S(2)}) collective-permute-start(bf16[1408,1024]{1,0:T(8,128)(2,1)} %down_grad_other.1), channel_id=1, source_target_pairs={{0,4},{4,0},{8,12},{12,8},{16,20},{20,16},{24,28},{28,24},{1,5},{5... | collective-permute-start | bytes 8650760 | tf_op jit(solution)/shard_map/ppermute | solution.py:79
  297.0 213.4 %reduce-scatter.6.cloned.1.call-start = ((), (), s32[]{:S(2)}) async-start(), calls=%async_computation.8 | async-start | bytes 7208960 | tf_op jit(solution)/shard_map/reduce_scatter | solution.py:1185
  319.8 265.8 %reduce-scatter.8.cloned.1.call-start = ((), (), s32[]{:S(2)}) async-start(), calls=%async_computation.9 | async-start | bytes 4587520 | tf_op jit(solution)/shard_map/reduce_scatter | solution.py:1185
  335.2 20.6 %collective-permute-start.26 = (bf16[192,2048]{1,0:T(8,128)(2,1)}, bf16[192,2048]{1,0:T(8,128)(2,1)S(1)}, u32[]{:S(2)}, u32[]{:S(2)}) collective-permute-start(bf16[192,2048]{1,0:T(8,128)(2,1)} %get-tuple-element.155), channel_id=1, source_target_pairs={{0,8},{4,12},{8,0},{12,4},{16,24},{20,28},{24,16},{28,20},{1,9},{5... | collective-permute-start | bytes 2359304 | tf_op jit(solution)/shard_map/ppermute | solution.py:79
  336.7 36.8 %collective-permute-start.27 = (bf16[192,2048]{1,0:T(8,128)(2,1)}, bf16[192,2048]{1,0:T(8,128)(2,1)}, u32[]{:S(2)}, u32[]{:S(2)}) collective-permute-start(bf16[192,2048]{1,0:T(8,128)(2,1)} %get-tuple-element.156), channel_id=1, source_target_pairs={{0,16},{4,20},{8,24},{12,28},{16,0},{20,4},{24,8},{28,12},{1,17},{... | collective-permute-start | bytes 2359304 | tf_op jit(solution)/shard_map/ppermute | solution.py:79
  338.1 35.3 %collective-permute-start.28 = (bf16[192,2048]{1,0:T(8,128)(2,1)}, bf16[192,2048]{1,0:T(8,128)(2,1)}, u32[]{:S(2)}, u32[]{:S(2)}) collective-permute-start(bf16[192,2048]{1,0:T(8,128)(2,1)} %get-tuple-element.157), channel_id=1, source_target_pairs={{0,24},{4,28},{8,16},{12,20},{16,8},{20,12},{24,0},{28,4},{1,25},{... | collective-permute-start | bytes 2359304 | tf_op jit(solution)/shard_map/ppermute | solution.py:79
  379.4 19.1 %collective-permute-start.29 = (bf16[192,2048]{1,0:T(8,128)(2,1)S(1)}, bf16[192,2048]{1,0:T(8,128)(2,1)}, u32[]{:S(2)}, u32[]{:S(2)}) collective-permute-start(bf16[192,2048]{1,0:T(8,128)(2,1)S(1)} %get-tuple-element.175.branch), channel_id=1, source_target_pairs={{0,8},{4,12},{8,0},{12,4},{16,24},{20,28},{24,16},{28,20},{1,9},{5... | collective-permute-start | bytes 2359304 | tf_op jit(solution)/shard_map/ppermute | solution.py:79
  425.1 27.2 %collective-permute-start.32 = (bf16[192,2048]{1,0:T(8,128)(2,1)S(1)}, bf16[192,2048]{1,0:T(8,128)(2,1)S(1)}, u32[]{:S(2)}, u32[]{:S(2)}) collective-permute-start(bf16[192,2048]{1,0:T(8,128)(2,1)S(1)} %copy-done.72), channel_id=1, source_target_pairs={{0,24},{4,28},{8,16},{12,20},{16,8},{20,12},{24,0},{28,4},{1,25},{... | collective-permute-start | bytes 2359304 | tf_op jit(solution)/shard_map/ppermute | solution.py:79
  427.8 24.6 %collective-permute-start.35 = (bf16[384,256]{1,0:T(8,128)(2,1)S(1)}, bf16[384,256]{1,0:T(8,128)(2,1)S(1)}, u32[]{:S(2)}, u32[]{:S(2)}) collective-permute-start(bf16[384,256]{1,0:T(8,128)(2,1)S(1)} %get-tuple-element.220), channel_id=1, source_target_pairs={{1,0},{2,1},{3,2},{5,4},{6,5},{7,6},{9,8},{10,9},{11,10},{13,12},{... | collective-permute-start | bytes 589832 | tf_op jit(solution)/shard_map/ppermute | solution.py:85
  429.1 39.4 %collective-permute-start.36 = (bf16[384,256]{1,0:T(8,128)(2,1)S(1)}, bf16[384,256]{1,0:T(8,128)(2,1)S(1)}, u32[]{:S(2)}, u32[]{:S(2)}) collective-permute-start(bf16[384,256]{1,0:T(8,128)(2,1)S(1)} %get-tuple-element.219), channel_id=1, source_target_pairs={{2,0},{3,1},{6,4},{7,5},{10,8},{11,9},{14,12},{15,13},{18,16},{19,... | collective-permute-start | bytes 589832 | tf_op jit(solution)/shard_map/ppermute | solution.py:85
  474.1 29.0 %collective-permute-start.38 = (bf16[1024,640]{1,0:T(8,128)(2,1)S(1)}, bf16[1024,640]{1,0:T(8,128)(2,1)S(1)}, u32[]{:S(2)}, u32[]{:S(2)}) collective-permute-start(bf16[1024,640]{1,0:T(8,128)(2,1)S(1)} %qkv_grad_other.3), channel_id=1, source_target_pairs={{0,4},{4,0},{8,12},{12,8},{16,20},{20,16},{24,28},{28,24},{1,5},{5... | collective-permute-start | bytes 3932168 | tf_op jit(solution)/shard_map/ppermute | solution.py:79
  476.3 30.5 %collective-permute-start.37 = (bf16[1024,640]{1,0:T(8,128)(2,1)S(1)}, bf16[1024,640]{1,0:T(8,128)(2,1)S(1)}, u32[]{:S(2)}, u32[]{:S(2)}) collective-permute-start(bf16[1024,640]{1,0:T(8,128)(2,1)S(1)} %qkv_grad_other.2), channel_id=1, source_target_pairs={{0,4},{4,0},{8,12},{12,8},{16,20},{20,16},{24,28},{28,24},{1,5},{5... | collective-permute-start | bytes 3932168 | tf_op jit(solution)/shard_map/ppermute | solution.py:79
  478.2 24.9 %collective-permute-start.40 = (bf16[256,1024]{1,0:T(8,128)(2,1)S(1)}, bf16[256,1024]{1,0:T(8,128)(2,1)S(1)}, u32[]{:S(2)}, u32[]{:S(2)}) collective-permute-start(bf16[256,1024]{1,0:T(8,128)(2,1)S(1)} %get-tuple-element.185), channel_id=1, source_target_pairs={{0,16},{4,20},{8,24},{12,28},{16,0},{20,4},{24,8},{28,12},{1,17},{... | collective-permute-start | bytes 1572872 | tf_op jit(solution)/shard_map/ppermute | solution.py:79
  479.0 31.4 %collective-permute-start.42 = (bf16[256,1024]{1,0:T(8,128)(2,1)}, bf16[256,1024]{1,0:T(8,128)(2,1)}, u32[]{:S(2)}, u32[]{:S(2)}) collective-permute-start(bf16[256,1024]{1,0:T(8,128)(2,1)} %get-tuple-element.192), channel_id=1, source_target_pairs={{0,24},{4,28},{8,16},{12,20},{16,8},{20,12},{24,0},{28,4},{1,25},{... | collective-permute-start | bytes 1572872 | tf_op jit(solution)/shard_map/ppermute | solution.py:79
  519.7 29.4 %collective-permute-start.45 = (bf16[256,2816]{1,0:T(8,128)(2,1)}, bf16[256,2816]{1,0:T(8,128)(2,1)}, u32[]{:S(2)}, u32[]{:S(2)}) collective-permute-start(bf16[256,2816]{1,0:T(8,128)(2,1)} %reduce-scatter.6.cloned.1.call-done.refs_0_), channel_id=1, source_target_pairs={{0,8},{4,12},{8,0},{12,4},{16,24},{20,28},{24,16},{28,20},{1,9},{5... | collective-permute-start | bytes 4325384 | tf_op jit(solution)/shard_map/ppermute | solution.py:79
  520.4 31.0 %collective-permute-start.47 = (bf16[256,2816]{1,0:T(8,128)(2,1)}, bf16[256,2816]{1,0:T(8,128)(2,1)}, u32[]{:S(2)}, u32[]{:S(2)}) collective-permute-start(bf16[256,2816]{1,0:T(8,128)(2,1)} %reduce-scatter.6.cloned.1.call-done.refs_0_), channel_id=1, source_target_pairs={{0,16},{4,20},{8,24},{12,28},{16,0},{20,4},{24,8},{28,12},{1,17},{... | collective-permute-start | bytes 4325384 | tf_op jit(solution)/shard_map/ppermute | solution.py:79
  558.8 27.9 %collective-permute-start.44 = (bf16[256,2816]{1,0:T(8,128)(2,1)}, bf16[256,2816]{1,0:T(8,128)(2,1)S(1)}, u32[]{:S(2)}, u32[]{:S(2)}) collective-permute-start(bf16[256,2816]{1,0:T(8,128)(2,1)} %reduce-scatter.6.cloned.1.call-done.refs_0_), channel_id=1, source_target_pairs={{0,4},{4,0},{8,12},{12,8},{16,20},{20,16},{24,28},{28,24},{1,5},{5... | collective-permute-start | bytes 4325384 | tf_op jit(solution)/shard_map/ppermute | solution.py:79
  558.8 29.4 %collective-permute-start.46 = (bf16[256,2816]{1,0:T(8,128)(2,1)}, bf16[256,2816]{1,0:T(8,128)(2,1)}, u32[]{:S(2)}, u32[]{:S(2)}) collective-permute-start(bf16[256,2816]{1,0:T(8,128)(2,1)} %collective-permute-done.45.refs_1_), channel_id=1, source_target_pairs={{0,4},{4,0},{8,12},{12,8},{16,20},{20,16},{24,28},{28,24},{1,5},{5... | collective-permute-start | bytes 4325384 | tf_op jit(solution)/shard_map/ppermute | solution.py:79
  559.3 29.5 %collective-permute-start.48 = (bf16[256,2816]{1,0:T(8,128)(2,1)}, bf16[256,2816]{1,0:T(8,128)(2,1)}, u32[]{:S(2)}, u32[]{:S(2)}) collective-permute-start(bf16[256,2816]{1,0:T(8,128)(2,1)} %collective-permute-done.47.refs_2_), channel_id=1, source_target_pairs={{0,4},{4,0},{8,12},{12,8},{16,20},{20,16},{24,28},{28,24},{1,5},{5... | collective-permute-start | bytes 4325384 | tf_op jit(solution)/shard_map/ppermute | solution.py:79
  561.7 21.2 %collective-permute-start.41 = (bf16[192,2048]{1,0:T(8,128)(2,1)S(1)}, bf16[192,2048]{1,0:T(8,128)(2,1)S(1)}, u32[]{:S(2)}, u32[]{:S(2)}) collective-permute-start(bf16[192,2048]{1,0:T(8,128)(2,1)S(1)} %get-tuple-element.189), channel_id=1, source_target_pairs={{0,8},{4,12},{8,0},{12,4},{16,24},{20,28},{24,16},{28,20},{1,9},{5... | collective-permute-start | bytes 2359304 | tf_op jit(solution)/shard_map/ppermute | solution.py:79
  567.0 31.5 %collective-permute-start.53 = (bf16[352,1024]{1,0:T(8,128)(2,1)}, bf16[352,1024]{1,0:T(8,128)(2,1)}, u32[]{:S(2)}, u32[]{:S(2)}) collective-permute-start(bf16[352,1024]{1,0:T(8,128)(2,1)} %reduce-scatter.4.cloned.1.call-done.refs_0_), channel_id=1, source_target_pairs={{0,8},{4,12},{8,0},{12,4},{16,24},{20,28},{24,16},{28,20},{1,9},{5... | collective-permute-start | bytes 2162696 | tf_op jit(solution)/shard_map/ppermute | solution.py:79
  582.9 46.2 %collective-permute-start.51 = (bf16[256,2816]{1,0:T(8,128)(2,1)}, bf16[256,2816]{1,0:T(8,128)(2,1)}, u32[]{:S(2)}, u32[]{:S(2)}) collective-permute-start(bf16[256,2816]{1,0:T(8,128)(2,1)} %constant_dynamic-update-slice_fusion.8.refs_3_), channel_id=1, source_target_pairs={{0,4},{4,0},{8,12},{12,8},{16,20},{20,16},{24,28},{28,24},{1,5},{5... | collective-permute-start | bytes 4325384 | tf_op jit(solution)/shard_map/ppermute | solution.py:79
  586.6 25.1 %collective-permute-start.43 = (bf16[256,640]{1,0:T(8,128)(2,1)S(1)}, bf16[256,640]{1,0:T(8,128)(2,1)S(1)}, u32[]{:S(2)}, u32[]{:S(2)}) collective-permute-start(bf16[256,640]{1,0:T(8,128)(2,1)S(1)} %slice.43), channel_id=1, source_target_pairs={{0,16},{4,20},{8,24},{12,28},{16,0},{20,4},{24,8},{28,12},{1,17},{... | collective-permute-start | bytes 983048 | tf_op jit(solution)/shard_map/ppermute | solution.py:79
  588.2 38.7 %collective-permute-start.55 = (bf16[352,1024]{1,0:T(8,128)(2,1)}, bf16[352,1024]{1,0:T(8,128)(2,1)S(1)}, u32[]{:S(2)}, u32[]{:S(2)}) collective-permute-start(bf16[352,1024]{1,0:T(8,128)(2,1)} %reduce-scatter.4.cloned.1.call-done.refs_0_), channel_id=1, source_target_pairs={{0,16},{4,20},{8,24},{12,28},{16,0},{20,4},{24,8},{28,12},{1,17},{... | collective-permute-start | bytes 2162696 | tf_op jit(solution)/shard_map/ppermute | solution.py:79
  588.7 38.2 %collective-permute-start.57 = (bf16[352,1024]{1,0:T(8,128)(2,1)}, bf16[352,1024]{1,0:T(8,128)(2,1)S(1)}, u32[]{:S(2)}, u32[]{:S(2)}) collective-permute-start(bf16[352,1024]{1,0:T(8,128)(2,1)} %reduce-scatter.4.cloned.1.call-done.refs_0_), channel_id=1, source_target_pairs={{0,24},{4,28},{8,16},{12,20},{16,8},{20,12},{24,0},{28,4},{1,25},{... | collective-permute-start | bytes 2162696 | tf_op jit(solution)/shard_map/ppermute | solution.py:79
  598.5 29.1 %collective-permute-start.52 = (bf16[352,1024]{1,0:T(8,128)(2,1)}, bf16[352,1024]{1,0:T(8,128)(2,1)S(1)}, u32[]{:S(2)}, u32[]{:S(2)}) collective-permute-start(bf16[352,1024]{1,0:T(8,128)(2,1)} %reduce-scatter.4.cloned.1.call-done.refs_0_), channel_id=1, source_target_pairs={{0,4},{4,0},{8,12},{12,8},{16,20},{20,16},{24,28},{28,24},{1,5},{5... | collective-permute-start | bytes 2162696 | tf_op jit(solution)/shard_map/ppermute | solution.py:79
  626.9 29.1 %collective-permute-start.56 = (bf16[352,1024]{1,0:T(8,128)(2,1)S(1)}, bf16[352,1024]{1,0:T(8,128)(2,1)S(1)}, u32[]{:S(2)}, u32[]{:S(2)}) collective-permute-start(bf16[352,1024]{1,0:T(8,128)(2,1)S(1)} %collective-permute-done.55.refs_4_), channel_id=1, source_target_pairs={{0,4},{4,0},{8,12},{12,8},{16,20},{20,16},{24,28},{28,24},{1,5},{5... | collective-permute-start | bytes 2162696 | tf_op jit(solution)/shard_map/ppermute | solution.py:79
  626.9 29.1 %collective-permute-start.58 = (bf16[352,1024]{1,0:T(8,128)(2,1)S(1)}, bf16[352,1024]{1,0:T(8,128)(2,1)S(1)}, u32[]{:S(2)}, u32[]{:S(2)}) collective-permute-start(bf16[352,1024]{1,0:T(8,128)(2,1)S(1)} %collective-permute-done.57.refs_6_), channel_id=1, source_target_pairs={{0,4},{4,0},{8,12},{12,8},{16,20},{20,16},{24,28},{28,24},{1,5},{5... | collective-permute-start | bytes 2162696 | tf_op jit(solution)/shard_map/ppermute | solution.py:79
  627.5 37.8 %collective-permute-start.60 = (bf16[256,1152]{1,0:T(8,128)(2,1)S(1)}, bf16[256,1152]{1,0:T(8,128)(2,1)S(1)}, u32[]{:S(2)}, u32[]{:S(2)}) collective-permute-start(bf16[256,1152]{1,0:T(8,128)(2,1)S(1)} %pad_maximum_fusion.1.refs_0_), channel_id=1, source_target_pairs={{0,8},{4,12},{8,0},{12,4},{16,24},{20,28},{24,16},{28,20},{1,9},{5... | collective-permute-start | bytes 1769480 | tf_op jit(solution)/shard_map/ppermute | solution.py:79
  629.1 36.8 %collective-permute-start.62 = (bf16[256,1152]{1,0:T(8,128)(2,1)S(1)}, bf16[256,1152]{1,0:T(8,128)(2,1)}, u32[]{:S(2)}, u32[]{:S(2)}) collective-permute-start(bf16[256,1152]{1,0:T(8,128)(2,1)S(1)} %pad_maximum_fusion.1.refs_0_), channel_id=1, source_target_pairs={{0,16},{4,20},{8,24},{12,28},{16,0},{20,4},{24,8},{28,12},{1,17},{... | collective-permute-start | bytes 1769480 | tf_op jit(solution)/shard_map/ppermute | solution.py:79
  630.6 35.4 %collective-permute-start.64 = (bf16[256,1152]{1,0:T(8,128)(2,1)S(1)}, bf16[256,1152]{1,0:T(8,128)(2,1)}, u32[]{:S(2)}, u32[]{:S(2)}) collective-permute-start(bf16[256,1152]{1,0:T(8,128)(2,1)S(1)} %pad_maximum_fusion.1.refs_0_), channel_id=1, source_target_pairs={{0,24},{4,28},{8,16},{12,20},{16,8},{20,12},{24,0},{28,4},{1,25},{... | collective-permute-start | bytes 1769480 | tf_op jit(solution)/shard_map/ppermute | solution.py:79
  (99 other events, 1085.0 us)
Sparse Core Ops, SparseCore 0:
  13.1 35.3 all-gather.4
  50.6 27.8 all-gather.6
  80.7 113.7 all-gather.8
  202.7 63.1 all-gather.10
  297.1 54.8 reduce-scatter.3
  354.7 114.2 reduce-scatter.5
  519.9 65.6 reduce-scatter.7
